TPU v7x, 32 devices: a whole 2x2x4 slice. The times are simulated.
32 devices in a mesh: pool: 2 (over x), slab: 8 (over z, y), ch: 2 (over core).
Axes of the slice: x: 2, y: 2, z: 4, core: 2. Of those that a mesh axis runs over, the one named last changes fastest.
Arguments:
- fields: bfloat16 [2, 20, 256, 224, 128], P('pool', 'ch', 'slab'), may hold values from -6 to 6
- mode_weights: bfloat16 [2, 20, 20, 64, 4096], P('pool', 'ch', None, None, 'slab'), may hold values from -1.25 to 1.25
- lin_weights: bfloat16 [2, 20, 20], P('pool', None, 'ch'), may hold values from -1.25 to 1.25
- bias: bfloat16 [2, 20], P('pool', 'ch'), may hold values from -1 to 1
- source: int32 [8, 8], P('slab'), may hold values from -1 to 7, as said below
Outputs:
- fields_out: bfloat16 [2, 20, 256, 224, 128], P('pool', 'ch', 'slab')
Inputs may be any that keep to these rules, and one draw needn't show every extreme that they name: source[s, b] is -1 (block not listed) or one of s - 1, s, s + 1; each row holds at most 2 entries equal to s - 1 and at most 2 equal to s + 1, and some row holds exactly 2 of each.
All inputs are finite; a program needn't handle non-finite values.
Results may differ from a plain program's by a relative error of at most 0.0055.
Values may be sent and summed in bfloat16 or wider, within the bound.
No kernel may reach another device: no remote copies, remote signals or barrier semaphores. Data moves between devices by JAX's collectives and lax.ppermute only.
A program may use at most 320 MiB of HBM per device.

v0:
```python
import jax
import jax.numpy as jnp
from jax import lax
from jax.sharding import PartitionSpec as P

HOP = 2


def shifted(value, axis, steps):
    count = lax.axis_size(axis)
    leading, last = (max(0, -steps), min(count, count - steps))
    return lax.ppermute(value, axis, [(source, source + steps) for source in range(leading, last)])


def swapped(value, axis, apart):
    mask = 2**apart
    pairs = [(source, source ^ mask) for source in range(lax.axis_size(axis))]
    return lax.ppermute(value, axis, pairs)


def tables(length, modes):
    cells = jnp.arange(length, dtype=jnp.float32)
    order = jnp.arange(modes, dtype=jnp.int32)
    half = modes // 2
    freq = jnp.where(order < half, order, order - half + 1).astype(jnp.float32)
    angle = 2.0 * jnp.pi * freq[:, None] * cells[None, :] / length
    forward = jnp.where((order < half)[:, None], jnp.cos(angle), jnp.sin(angle))
    return (forward.astype(jnp.bfloat16), (forward.T * (2.0 / length)).astype(jnp.bfloat16))


def interp_table(length):
    fine_idx = jnp.arange(length, dtype=jnp.int32)[:, None]
    coarse_idx = jnp.arange(length, dtype=jnp.int32)[None, :]
    centre = length // 4 + fine_idx // 2
    second = centre - 1 + 2 * (fine_idx % 2)
    return 0.75 * (coarse_idx == centre).astype(jnp.float32) + 0.25 * (coarse_idx == second).astype(
        jnp.float32
    )


def body(fields, mode_weights, lin_weights, bias, source):
    field = fields[0]
    mode_local = mode_weights[0]
    lin_local = lin_weights[0]
    bias_local = bias[0].astype(jnp.float32)
    own_row = source[0]
    own_ch, planes, y_cells, z_cells = field.shape
    modes = mode_local.shape[2]
    x_cells = planes * lax.axis_size("slab")
    block_count = own_row.shape[0]
    block_rows = y_cells // block_count
    slab_id = lax.axis_index("slab")
    is_coarse = lax.axis_index("pool") == 0
    fwd_x, inv_x = tables(x_cells, modes)
    fwd_y, inv_y = tables(y_cells, modes)
    fwd_z, inv_z = tables(z_cells, modes)
    pmat = interp_table(z_cells)
    z_table = jnp.where(is_coarse, pmat.T.astype(jnp.bfloat16), (0.5 * pmat).astype(jnp.bfloat16))
    block_ids = jnp.arange(block_count, dtype=jnp.int32)
    here_mask = (own_row == slab_id).astype(jnp.float32)[None, None, :, None]
    side_rows = [shifted(own_row, "slab", shift_by) for shift_by in (1, -1)]
    all_channels = lax.all_gather(field, "ch", axis=0, tiled=True)
    along_y = jnp.einsum("cxyz,my->cxmz", field, fwd_y, preferred_element_type=jnp.float32).astype(
        jnp.bfloat16
    )
    along_z = jnp.einsum(
        "cxmz,kz->cxmk", along_y, fwd_z, preferred_element_type=jnp.float32
    ).astype(jnp.bfloat16)
    along_z = along_z.reshape(own_ch, planes, modes * modes)
    pencils = lax.all_to_all(along_z, "slab", split_axis=2, concat_axis=1, tiled=True)
    coeffs = jnp.einsum("cxq,nx->cnq", pencils, fwd_x, preferred_element_type=jnp.float32).astype(
        jnp.bfloat16
    )
    partial_mix = jnp.einsum(
        "inq,ionq->onq", coeffs, mode_local, preferred_element_type=jnp.float32
    )
    mixed = lax.psum_scatter(
        partial_mix.astype(jnp.bfloat16), "ch", scatter_dimension=0, tiled=True
    )
    back_x = jnp.einsum("onq,xn->oxq", mixed, inv_x, preferred_element_type=jnp.float32).astype(
        jnp.bfloat16
    )
    back_x = lax.all_to_all(back_x, "slab", split_axis=1, concat_axis=2, tiled=True).reshape(
        own_ch, planes, modes, modes
    )
    back_z = jnp.einsum("cxmk,zk->cxmz", back_x, inv_z, preferred_element_type=jnp.float32).astype(
        jnp.bfloat16
    )
    spec = jnp.einsum("cxmz,ym->cxyz", back_z, inv_y, preferred_element_type=jnp.float32)
    flat_all = all_channels.reshape(all_channels.shape[0], planes * y_cells * z_cells)
    linear = jnp.einsum("io,ir->or", lin_local, flat_all, preferred_element_type=jnp.float32)
    linear = linear.reshape(own_ch, planes, y_cells, z_cells)
    anchor = jnp.where(is_coarse, field, spec.astype(jnp.bfloat16))
    payload = jnp.dot(anchor, z_table, preferred_element_type=jnp.float32).astype(jnp.bfloat16)
    partner = swapped(payload, "pool", 0)
    partner_blocks = partner.reshape(own_ch, planes, block_count, block_rows * z_cells)
    coupling = partner_blocks.astype(jnp.float32) * here_mask
    for shift_by, dest_row in ((1, side_rows[1]), (-1, side_rows[0])):
        sending = jnp.where(is_coarse, own_row == slab_id + shift_by, dest_row == slab_id).astype(
            jnp.int32
        )
        position = jnp.cumsum(sending) - 1
        slots = jnp.arange(HOP, dtype=jnp.int32)[:, None]
        select = (sending[None, :] == 1) & (position[None, :] == slots)
        packed = jnp.einsum(
            "hb,cxbr->cxhr",
            select.astype(jnp.bfloat16),
            partner_blocks,
            preferred_element_type=jnp.float32,
        ).astype(jnp.bfloat16)
        packed_ids = jnp.where(
            jnp.any(select, axis=1),
            jnp.sum(select.astype(jnp.int32) * block_ids[None, :], axis=1),
            -1,
        )
        arrived, arrived_ids = shifted((packed, packed_ids), "slab", shift_by)
        placing = (arrived_ids[:, None] == block_ids[None, :]).astype(jnp.bfloat16)
        coupling = coupling + jnp.einsum(
            "hb,cxhr->cxbr", placing, arrived, preferred_element_type=jnp.float32
        )
    total = (
        spec
        + linear
        + bias_local[:, None, None, None]
        + coupling.reshape(own_ch, planes, y_cells, z_cells)
    )
    field = jax.nn.gelu(total, approximate=False).astype(jnp.bfloat16)
    return field[None]


def solution(mesh):
    return jax.shard_map(
        body,
        mesh=mesh,
        in_specs=(
            P("pool", "ch", "slab", None, None),
            P("pool", "ch", None, None, "slab"),
            P("pool", None, "ch"),
            P("pool", "ch"),
            P("slab", None),
        ),
        out_specs=P("pool", "ch", "slab", None, None),
        check_vma=False,
    )
```

profile of v0, /device:TPU:18, one launch (start us, length us, event | category | flops | bytes accessed | tf_op | source)
XLA Modules:
  0.0 1181.1 jit_solution(105525995718668675)
XLA Ops:
  6.6 10.7 fusion.38
  17.2 18.5 %copy.39 = bf16[10,32,64,64]{1,0,3,2:T(8,128)(2,1)} copy(bf16[10,32,64,64]{3,2,1,0:T(8,128)(2,1)} %fusion.38) | data formatting | bytes 5242880 | tf_op jit(solution)/shard_map/reshape | solution.py:69
  35.7 13.2 %reshape.189 = bf16[8,2,81920]{2,1,0:T(2,128)(2,1)S(1)} reshape(bf16[4096,10,32]{2,1,0:T(8,128)(2,1)} %bitcast.182) | data formatting | bytes 5242880
  48.9 63.9 %all_to_all.33 = bf16[8,2,81920]{2,1,0:T(2,128)(2,1)} all-to-all(bf16[8,2,81920]{2,1,0:T(2,128)(2,1)S(1)} %reshape.189), channel_id=1, replica_groups=mesh['pool'=2,'slab'=8,'ch'=2] {'slab'}, dimensions={0} | all-to-all | bytes 5242880 | tf_op jit(solution)/shard_map/all_to_all | solution.py:70
  112.8 12.7 %reshape.190 = bf16[4096,10,32]{2,1,0:T(8,128)(2,1)} reshape(bf16[8,2,81920]{2,1,0:T(2,128)(2,1)} %all_to_all.33) | data formatting | bytes 5242880
  125.5 15.0 %copy.16 = bf16[10,8,32,512]{3,2,1,0:T(8,128)(2,1)S(1)} copy(bf16[10,8,32,512]{2,0,3,1:T(8,128)(2,1)} %bitcast.181) | data formatting | bytes 5242880 | tf_op jit(solution)/shard_map/all_to_all | solution.py:70
  142.4 9.6 multiply_reduce_fusion
  152.0 9.5 reduce-scatter.2.cloned.1.call-done
  161.5 2.3 convert_bitcast_fusion
  163.8 3.7 copy.17
  167.5 6.0 all-to-all-start.1
  174.3 89.6 %all-to-all-done.1 = bf16[10,256,512]{2,0,1:T(8,128)(2,1)} async-done(((bf16[10,256,512]{2,0,1:T(8,128)(2,1)}), bf16[10,256,512]{2,0,1:T(8,128)(2,1)}, u32[]{:S(2)}, u32[]{:S(2)}) %all-to-all-start.1) | async-done | bytes 2621472 | tf_op jit(solution)/shard_map/all_to_all | solution.py:83
  263.8 3.6 copy.53
  267.5 4.5 reshape.166
  272.0 17.2 %fusion.29 = f32[224,10,32,128]{3,0,2,1:T(8,128)} fusion(bf16[10,32,64,64]{3,2,1,0:T(8,128)(2,1)} %reshape.166, f32[64]{0:T(128)S(1)} %fusion.112, pred[64]{0:T(512)(128)(4,1)S(1)} %iota_compare_fusion.4), kind=kOutput, calls=%fused_computation.42 | convolution fusion | flops 1512683520 | bytes 39321920 | tf_op jit(solution)/shard_map/cxmz,ym->cxyz/dot_general | solution.py:89
  289.2 25.6 %fusion.22 = bf16[10,32,224,128]{3,2,1,0:T(8,128)(2,1)} fusion(f32[224,10,32,128]{3,0,2,1:T(8,128)} %fusion.29, bf16[1,10,32,224,128]{4,3,2,1,0:T(8,128)(2,1)} %param.5, pred[]{:T(512)S(6)} %eq.127, s32[128]{0:T(128)S(1)} %get-tuple-element.16, s32[128]{0:T(128)S(1)} %get-tuple-element.17), kind=kOutput, calls=%fused_computation.35 | convolution fusion | flops 2376564736 | bytes 73401344 | tf_op jit(solution)/shard_map/dot_general | solution.py:94
  315.3 3.4 collective-permute-start.1
  318.7 2.5 collective-permute-start.4
  321.2 3.8 collective-permute-done.4
  325.6 384.5 %collective-permute-done = bf16[10,32,224,128]{3,2,1,0:T(8,128)(2,1)} collective-permute-done((bf16[10,32,224,128]{3,2,1,0:T(8,128)(2,1)}, bf16[10,32,224,128]{3,2,1,0:T(8,128)(2,1)}, u32[]{:S(2)}, u32[]{:S(2)}) %collective-permute-start) | collective-permute-done | bytes 18350112 | tf_op jit(solution)/shard_map/ppermute | solution.py:18
  710.1 32.4 %reshape.168 = bf16[10,32,8,3584]{3,2,1,0:T(8,128)(2,1)} reshape(bf16[10,32,224,128]{3,2,1,0:T(8,128)(2,1)} %collective-permute-done) | data formatting | bytes 36700160 | tf_op jit(solution)/shard_map/reshape | solution.py:96
  742.5 10.6 fusion.25
  753.1 3.4 collective-permute-start.2
  756.5 10.7 fusion.26
  767.2 3.4 collective-permute-start.5
  770.8 4.6 collective-permute-start.3
  777.6 174.2 %collective-permute-done.3 = s32[2]{0:T(128)S(1)} collective-permute-done((s32[2]{0:T(128)S(1)}, s32[2]{0:T(128)S(1)}, u32[]{:S(2)}, u32[]{:S(2)}) %collective-permute-start.3) | collective-permute-done | bytes 40 | tf_op jit(solution)/shard_map/ppermute | solution.py:12
  951.8 14.9 %fusion.102 = f32[10,32,3584,8]{2,3,1,0:T(8,128)} fusion(bf16[10,32,2,3584]{3,2,1,0:T(2,128)(2,1)} %collective-permute-done.2, s32[2]{0:T(128)S(1)} %collective-permute-done.3), kind=kOutput, calls=%fused_computation.106 | convolution fusion | flops 36700176 | bytes 41287688 | tf_op jit(solution)/shard_map/hb,cxhr->cxbr/dot_general | solution.py:118
  966.7 33.6 %bitcast_add_fusion = f32[10,32,8,3584]{3,2,1,0:T(8,128)} fusion(f32[10,32,3584,8]{2,3,1,0:T(8,128)} %fusion.102, bf16[10,32,8,3584]{3,2,1,0:T(8,128)(2,1)} %reshape.168, f32[8]{0:T(128)S(1)} %get-tuple-element.15, bf16[10,32,2,3584]{3,2,1,0:T(2,128)(2,1)} %collective-permute-done.5, s32[2]{0:T(128)S(1)} %collective-permute-done.6), kind=kOutput, calls=%fused_computation.6 | convolution fusion | flops 73400336 | bytes 96337960 | tf_op jit(solution)/shard_map/hb,cxhr->cxbr/dot_general | solution.py:118
  1000.3 36.1 %reshape.171 = f32[10,32,224,128]{3,2,1,0:T(8,128)} reshape(f32[10,32,8,3584]{3,2,1,0:T(8,128)} %bitcast_add_fusion) | data formatting | bytes 73400320 | tf_op jit(solution)/shard_map/reshape | solution.py:125
  1036.4 45.9 %fusion = f32[10,32,224,128]{3,0,2,1:T(8,128)} fusion(bf16[32,224,128,20]{2,1,0,3:T(8,128)(2,1)} %bitcast.180, bf16[1,20,10]{1,2,0:T(8,128)(2,1)S(1)} %copy-done), kind=kOutput, calls=%fused_computation.1 | convolution fusion | flops 367001600 | bytes 73400720 | tf_op jit(solution)/shard_map/io,ir->or/dot_general | solution.py:91
  1082.3 91.5 %fusion.21 = bf16[1,10,32,224,128]{4,3,2,1,0:T(8,128)(2,1)} fusion(f32[10,32,224,128]{3,2,1,0:T(8,128)} %reshape.171, f32[10]{0:T(128)S(1)} %bitcast_convert_fusion.1, f32[10,32,224,128]{3,0,2,1:T(8,128)} %fusion, f32[224,10,32,128]{3,0,2,1:T(8,128)} %fusion.29), kind=kLoop, calls=%fused_computation.34 | loop fusion | flops 623902720 | bytes 128450600 | tf_op jit(solution)/shard_map/broadcast_in_dim | solution.py:128
  (32 shorter events, 6.1 us)
Async XLA Ops:
  6.5 1029.9 %copy-start = (bf16[1,20,10]{1,2,0:T(8,128)(2,1)S(1)}, bf16[1,20,10]{1,2,0:T(8,128)(2,1)}, u32[]{:S(2)}) copy-start(bf16[1,20,10]{1,2,0:T(8,128)(2,1)} %param.7) | copy-start | bytes 1204
  6.5 155.0 %reduce-scatter.2.cloned.1.call-start = ((), (), s32[]{:S(2)}) async-start(), calls=%async_computation.3 | async-start | bytes 1966080 | tf_op jit(solution)/shard_map/reduce_scatter | solution.py:77
  167.5 96.4 %all-to-all-start.1 = ((bf16[10,256,512]{2,0,1:T(8,128)(2,1)}), bf16[10,256,512]{2,0,1:T(8,128)(2,1)}, u32[]{:S(2)}, u32[]{:S(2)}) async-start(bf16[10,256,512]{2,0,1:T(8,128)(2,1)} %copy.17), calls=%async_computation.2 | async-start | bytes 8388608 | tf_op jit(solution)/shard_map/all_to_all | solution.py:83
  173.5 862.9 %all-gather.3.cloned.1.call-start = ((), (), s32[]{:S(2)}) async-start(), calls=%async_computation.4 | async-start | bytes 55050240 | tf_op jit(solution)/shard_map/all_gather | solution.py:62
  289.2 26.1 %copy-start.1 = (s32[1,8]{1,0:T(1,128)S(1)}, s32[1,8]{1,0:T(1,128)}, u32[]{:S(2)}) copy-start(s32[1,8]{1,0:T(1,128)} %param.9) | copy-start | bytes 100
  314.8 395.3 %collective-permute-start = (bf16[10,32,224,128]{3,2,1,0:T(8,128)(2,1)}, bf16[10,32,224,128]{3,2,1,0:T(8,128)(2,1)}, u32[]{:S(2)}, u32[]{:S(2)}) collective-permute-start(bf16[10,32,224,128]{3,2,1,0:T(8,128)(2,1)} %fusion.22), channel_id=1, source_target_pairs={{0,16},{16,0},{1,17},{17,1},{2,18},{18,2},{3,19},{19,3},{4,20},{20... | collective-permute-start | bytes 55050248 | tf_op jit(solution)/shard_map/ppermute | solution.py:18
  315.3 5.9 collective-permute-start.1
  318.7 6.3 collective-permute-start.4
  325.5 445.0 %copy-start.2 = (bf16[1,10]{1,0:T(2,128)(2,1)S(1)}, bf16[1,10]{1,0:T(2,128)(2,1)}, u32[]{:S(2)}) copy-start(bf16[1,10]{1,0:T(2,128)(2,1)} %param.8) | copy-start | bytes 64
  753.1 198.7 %collective-permute-start.2 = (bf16[10,32,2,3584]{3,2,1,0:T(2,128)(2,1)}, bf16[10,32,2,3584]{3,2,1,0:T(2,128)(2,1)}, u32[]{:S(2)}, u32[]{:S(2)}) collective-permute-start(bf16[10,32,2,3584]{3,2,1,0:T(2,128)(2,1)} %fusion.25), channel_id=1, source_target_pairs={{0,2},{2,4},{4,6},{6,8},{8,10},{10,12},{12,14},{1,3},{3,5},{5,7},{... | collective-permute-start | bytes 13762568 | tf_op jit(solution)/shard_map/ppermute | solution.py:12
  767.2 199.5 %collective-permute-start.5 = (bf16[10,32,2,3584]{3,2,1,0:T(2,128)(2,1)}, bf16[10,32,2,3584]{3,2,1,0:T(2,128)(2,1)}, u32[]{:S(2)}, u32[]{:S(2)}) collective-permute-start(bf16[10,32,2,3584]{3,2,1,0:T(2,128)(2,1)} %fusion.26), channel_id=1, source_target_pairs={{2,0},{4,2},{6,4},{8,6},{10,8},{12,10},{14,12},{3,1},{5,3},{7,5},{... | collective-permute-start | bytes 13762568 | tf_op jit(solution)/shard_map/ppermute | solution.py:12
  770.8 181.0 %collective-permute-start.3 = (s32[2]{0:T(128)S(1)}, s32[2]{0:T(128)S(1)}, u32[]{:S(2)}, u32[]{:S(2)}) collective-permute-start(s32[2]{0:T(128)S(1)} %broadcast_select_fusion.1), channel_id=1, source_target_pairs={{0,2},{2,4},{4,6},{6,8},{8,10},{10,12},{12,14},{1,3},{3,5},{5,7},{... | collective-permute-start | bytes 32 | tf_op jit(solution)/shard_map/ppermute | solution.py:12
  775.4 191.3 %collective-permute-start.6 = (s32[2]{0:T(128)S(1)}, s32[2]{0:T(128)S(1)}, u32[]{:S(2)}, u32[]{:S(2)}) collective-permute-start(s32[2]{0:T(128)S(1)} %broadcast_select_fusion), channel_id=1, source_target_pairs={{2,0},{4,2},{6,4},{8,6},{10,8},{12,10},{14,12},{3,1},{5,3},{7,5},{... | collective-permute-start | bytes 32 | tf_op jit(solution)/shard_map/ppermute | solution.py:12
Sparse Core Ops, SparseCore 0:
  152.1 9.3 reduce-scatter.1
  176.0 57.9 all-gather.2
where the time goes:
time: 1190 us; the launch traced here: 1180 us
  waiting for transfers between devices  662 us (56%)
  matrix products  173 us (15%)
  local copies, waits for them, and re-layouts  140 us (12%)
  other arithmetic  102 us (9%)
  blocking collectives  63.9 us (5%)
  starting transfers between devices  26.1 us (2%)
  between operations  14 us (1%)
    ppermute x1, waiting for transfers between devices, swapped(): return lax.ppermute(value, axis, pairs)  385 us
    ppermute x6, waiting for transfers between devices, shifted(): lax.ppermute(value, axis, [(source, source + steps) for source in range(l...  178 us
    broadcast_in_dim x1, other arithmetic, body(): return field[None]  91.5 us
    all_to_all x1, waiting for transfers between devices, body(): lax.all_to_all(back_x, 'slab', split_axis=1, concat_axis=2, tiled=True)  89.6 us
    all_to_all x1, blocking collectives, body(): lax.all_to_all(along_z, 'slab', split_axis=2, concat_axis=1, tiled=True)  63.9 us
    dot_general x2, matrix products, body(): jnp.einsum('hb,cxhr->cxbr', placing, arrived, preferred_element_type=jnp....  48.5 us
    dot_general x1, matrix products, body(): jnp.einsum('io,ir->or', lin_local, flat_all, preferred_element_type=jnp.f...  45.9 us
    reshape x1, local copies, waits for them, and re-layouts, body(): coupling.reshape(own_ch, planes, y_cells, z_cells)  36.1 us
  transfers between devices with their start and end apart: 10, of which 5 were waited for; matrix products, arithmetic and copies ran while one was open for 16% of the time, Pallas kernels for 0%

commit v1 on v0

--- a/solution.py
+++ b/solution.py
@@ -1,9 +1,22 @@
+import functools
+
 import jax
 import jax.numpy as jnp
+import ml_dtypes
+import numpy as np
 from jax import lax
+from jax.experimental import pallas as pl
+from jax.experimental.pallas import tpu as pltpu
 from jax.sharding import PartitionSpec as P
 
 HOP = 2
+LANES = 128
+BF = jnp.bfloat16
+F32 = jnp.float32
+ERF_POLY = (
+    7.97884216e-01, 3.63342835e-02, -3.31299940e-05, -5.52401584e-05,
+    3.96910946e-06, -1.33446410e-07, 1.80561642e-09,
+)
 
 
 def shifted(value, axis, steps):
@@ -38,12 +51,701 @@
     )
 
 
-def body(fields, mode_weights, lin_weights, bias, source):
-    field = fields[0]
-    mode_local = mode_weights[0]
-    lin_local = lin_weights[0]
-    bias_local = bias[0].astype(jnp.float32)
-    own_row = source[0]
+def host_interp(length):
+    fine = np.arange(length)[:, None]
+    coarse = np.arange(length)[None, :]
+    centre = length // 4 + fine // 2
+    second = centre - 1 + 2 * (fine % 2)
+    return (0.75 * (coarse == centre) + 0.25 * (coarse == second)).astype(np.float32)
+
+
+def host_tables(length, modes):
+    cells = np.arange(length, dtype=np.float32)
+    order = np.arange(modes)
+    half = modes // 2
+    freq = np.where(order < half, order, order - half + 1).astype(np.float32)
+    angle = np.float32(2.0 * np.pi) * freq[:, None] * cells[None, :] / np.float32(length)
+    forward = np.where((order < half)[:, None], np.cos(angle), np.sin(angle)).astype(np.float32)
+    inverse = forward.T * np.float32(2.0 / length)
+    return forward.astype(ml_dtypes.bfloat16), inverse.astype(ml_dtypes.bfloat16)
+
+
+def two_of(table):
+    zero = np.zeros_like(table)
+    return np.block([[table, zero], [zero, table]])
+
+
+def dot(left, right):
+    return jnp.dot(left, right, preferred_element_type=F32)
+
+
+def gelu(v):
+    square = jnp.minimum(v * v, 36.0)
+    poly = ERF_POLY[-1]
+    for coef in ERF_POLY[-2::-1]:
+        poly = poly * square + coef
+    half = 0.5 * v
+    return half + half * jnp.tanh(v * poly)
+
+
+class Plan:
+    def __init__(self, field, mode_local, own_row, slabs):
+        self.ch, self.planes, self.ny, self.nz = field.shape
+        self.modes, self.q = mode_local.shape[2], mode_local.shape[3]
+        self.outs = mode_local.shape[1]
+        self.blocks = own_row.shape[0]
+        self.slabs = slabs
+        self.nx = self.planes * slabs
+        self.rows = self.ny // self.blocks
+        self.half = (self.blocks - 2 * HOP) * self.rows
+        self.hop = HOP * self.rows
+        self.group = self.modes // slabs if self.modes % slabs == 0 else 0
+        self.pairs = self.planes // 2
+        self.mid_rows = 2 * self.pairs * self.half
+        self.pack_rows = self.mid_rows + self.half
+        self.edge_rows = -(-self.hop // 16) * 16
+        self.nb_rows = self.pairs * 2 * self.hop + self.edge_rows
+        total = self.ch // 2
+        counts = [-(-total // 2), total // 2]
+        self.groups = [(sum(counts[:i]), count) for i, count in enumerate(counts) if count]
+        self.step = self.planes + 8 if self.planes % 16 == 0 else self.planes
+        self.depth = 4 * self.modes + 8
+
+    def chan_spec(self):
+        return pl.BlockSpec((1, self.planes, self.ny, self.nz), lambda c: (c, 0, 0, 0))
+
+    def fits(self):
+        return (
+            self.group >= 2
+            and self.group % 2 == 0
+            and self.slabs & (self.slabs - 1) == 0
+            and self.nz == LANES
+            and 2 * self.modes == LANES
+            and self.ch % 2 == 0
+            and self.outs == 2 * self.ch
+            and self.planes % 16 == 0
+            and 4 * self.planes <= LANES
+            and self.ny % 16 == 0
+            and self.blocks == 4 * HOP
+            and self.half % 16 == 0
+            and self.half == 2 * self.hop
+            and self.hop % 8 == 0
+            and self.hop <= 64
+            and self.q == self.group * self.modes
+        )
+
+
+def listing(meta, plan):
+    nb = plan.blocks
+    slab = meta[3 * nb]
+    one, zero = jnp.int32(1), jnp.int32(0)
+    row = [meta[b] for b in range(nb)]
+    left = [jnp.where((row[b] == slab - 1) & (row[b] >= 0), one, zero) for b in range(nb)]
+    right = [jnp.where(row[b] == slab + 1, one, zero) for b in range(nb)]
+    listed = [jnp.where(row[b] >= 0, one, zero) for b in range(nb)]
+    near = [1 - left[b] - right[b] for b in range(nb)]
+    total = functools.reduce(lambda a, b: a + b, near)
+    place, rank_l, rank_r = [], [], []
+    n_near, n_far, n_l, n_r = zero, total, zero, zero
+    for b in range(nb):
+        place.append(jnp.where(near[b] == 1, n_near, n_far))
+        rank_l.append(n_l)
+        rank_r.append(n_r)
+        n_near, n_far = n_near + near[b], n_far + 1 - near[b]
+        n_l, n_r = n_l + left[b], n_r + right[b]
+    return dict(slab=slab, left=left, right=right, listed=listed, near=near, place=place,
+                rank_l=rank_l, rank_r=rank_r)
+
+
+def sends(meta, plan, which):
+    nb = plan.blocks
+    slab = meta[3 * nb]
+    ask = [jnp.where(meta[which * nb + b] == slab, jnp.int32(1), jnp.int32(0)) for b in range(nb)]
+    rank, count = [], jnp.int32(0)
+    for b in range(nb):
+        rank.append(jnp.where(ask[b] == 1, count, jnp.int32(-1)))
+        count = count + ask[b]
+    return rank
+
+
+def steps_of(index, size, count):
+    out = jnp.zeros_like(index)
+    for k in range(1, count):
+        out = out + jnp.where(index >= k * size, jnp.int32(1), jnp.int32(0))
+    return out
+
+
+def by_block(block, values):
+    out = jnp.full_like(block, -1)
+    for b, value in enumerate(values):
+        out = jnp.where(block == b, value, out)
+    return out
+
+
+def chosen(mask):
+    return jnp.where(mask, 1.0, 0.0).astype(F32)
+
+
+def row_col(rows, cols):
+    shape = (rows, cols)
+    return lax.broadcasted_iota(jnp.int32, shape, 0), lax.broadcasted_iota(jnp.int32, shape, 1)
+
+
+def forward_kernel(plan, fy, fz2, u, out, scr):
+    planes, modes, step = plan.planes, plan.modes, plan.step
+    for xp in range(plan.pairs):
+        both = jnp.concatenate([u[0, 2 * xp], u[0, 2 * xp + 1]], axis=1)
+        along = dot(fy[...], both)
+        for side in range(2):
+            scr[pl.ds(2 * xp + side, modes, stride=step), :] = along[
+                :, side * LANES:(side + 1) * LANES
+            ]
+    for d in range(plan.slabs):
+        lefts = []
+        for jp in range(plan.group // 2):
+            start = (d * plan.group + 2 * jp) * step
+            lefts.append(jnp.concatenate(
+                [scr[start:start + planes], scr[start + step:start + step + planes]], axis=1
+            ))
+        done = dot(jnp.concatenate(lefts, axis=0).astype(BF), fz2[...]).astype(BF)
+        for jp in range(plan.group // 2):
+            out[d, 0, :, jp * LANES:(jp + 1) * LANES] = done[jp * planes:(jp + 1) * planes]
+
+
+def pack(plan, sel, esel, u, store, store_edges):
+    lo, mid = plan.nz // 4, plan.nz // 2
+    edges = jnp.zeros((plan.ny, LANES), F32)
+    for c2 in range(2):
+        for double in range(plan.pairs // 2):
+            mids = []
+            for i in range(2):
+                x = 4 * double + 2 * i
+                mids += [u[c2, x, :, lo:lo + mid], u[c2, x + 1, :, lo:lo + mid]]
+            packed = dot(sel[...], jnp.concatenate(mids, axis=1))
+            store(c2, double, [packed[:, :LANES], packed[:, LANES:]])
+        for xp in range(plan.pairs):
+            both = jnp.concatenate([u[c2, 2 * xp], u[c2, 2 * xp + 1]], axis=1)
+            edges = edges + dot(both, esel[c2 * plan.pairs + xp])
+    store_edges(dot(sel[...], edges.astype(BF)).astype(BF))
+
+
+def picks(plan, info, first):
+    nb = plan.blocks
+    row, col = row_col(plan.half, plan.ny)
+    block = steps_of(col, plan.rows, nb)
+    slot = steps_of(row, plan.rows, 2 * HOP) + first
+    same = row - (slot - first) * plan.rows == col - block * plan.rows
+    near = by_block(block, info["near"]) == 1
+    return chosen(same & near & (by_block(block, info["place"]) == slot)).astype(BF)
+
+
+def pack_first_kernel(plan, meta, esel, u, h1, sel):
+    half = plan.half
+
+    @pl.when(pl.program_id(0) == 0)
+    def _():
+        sel[...] = picks(plan, listing(meta, plan), 0)
+
+    def store(c2, double, tiles):
+        for i, tile in enumerate(tiles):
+            at = (c2 * plan.pairs + 2 * double + i) * half
+            h1[0, at:at + half, :] = tile.astype(BF)
+
+    def store_edges(packed):
+        h1[0, plan.mid_rows:] = packed
+
+    pack(plan, sel, esel, u, store, store_edges)
+
+
+def pack_rest_kernel(plan, meta, esel, u, h2, right, left, sel):
+    half, hop, nb = plan.half, plan.hop, plan.blocks
+    pad = plan.edge_rows
+
+    @pl.when(pl.program_id(0) == 0)
+    def _():
+        sel[0:half] = picks(plan, listing(meta, plan), nb - 2 * HOP)
+        row, col = row_col(pad, plan.ny)
+        block = steps_of(col, plan.rows, nb)
+        slot = steps_of(row, plan.rows, HOP + 1)
+        same = (row - slot * plan.rows == col - block * plan.rows) & (slot < HOP)
+        for which in range(2):
+            rank = by_block(block, sends(meta, plan, 2 - which))
+            start = half + which * pad
+            sel[start:start + pad] = chosen(same & (rank == slot)).astype(BF)
+
+    def store(c2, double, tiles):
+        for i, tile in enumerate(tiles):
+            at = (c2 * plan.pairs + 2 * double + i) * half
+            h2[0, at:at + half, :] = tile[0:half].astype(BF)
+        at = (c2 * plan.pairs // 2 + double) * 2 * hop
+        for ref, start in ((right, half), (left, half + pad)):
+            ref[0, at:at + 2 * hop, :] = jnp.concatenate(
+                [tile[start:start + hop] for tile in tiles], axis=0
+            ).astype(BF)
+
+    def store_edges(packed):
+        h2[0, plan.mid_rows:] = packed[0:half]
+        right[0, 2 * plan.pairs * hop:] = packed[half:half + pad]
+        left[0, 2 * plan.pairs * hop:] = packed[half + pad:half + 2 * pad]
+
+    pack(plan, sel, esel, u, store, store_edges)
+
+
+def assemble_kernel(plan, meta, h2, from_left, from_right, out, sel, edge_sel):
+    half, hop, nb = plan.half, plan.hop, plan.blocks
+    pad = plan.edge_rows
+
+    @pl.when(pl.program_id(0) == 0)
+    def _():
+        info = listing(meta, plan)
+
+        def build(width, period, offset):
+            row, col = row_col(half, 2 * width)
+            side = steps_of(col, width, 2)
+            within = col - side * width
+            part = steps_of(within, period, max(1, width // period))
+            inner = within - part * period
+            slot = steps_of(inner, plan.rows, HOP + 1)
+            target = steps_of(row, plan.rows, 2 * HOP)
+            same = (row - target * plan.rows == inner - slot * plan.rows) & (part == offset)
+            mask = jnp.zeros((half, 2 * width), F32)
+            for b in range(nb):
+                place = info["place"][b] - (nb - 2 * HOP)
+                hit = same & (target == place)
+                mask = mask + chosen(
+                    hit & (side == 0) & (slot == info["rank_l"][b]) & (info["left"][b] == 1)
+                ) + chosen(
+                    hit & (side == 1) & (slot == info["rank_r"][b]) & (info["right"][b] == 1)
+                )
+            return mask.astype(BF)
+
+        for offset in range(2):
+            sel[offset] = build(2 * hop, hop, offset)
+        edge_sel[...] = build(pad, pad, 0)
+
+    @pl.loop(0, plan.pairs, unroll=4)
+    def _(double):
+        at = pl.multiple_of(double * 2 * hop, 16)
+        sides = jnp.concatenate(
+            [from_left[0, pl.ds(at, 2 * hop), :], from_right[0, pl.ds(at, 2 * hop), :]], axis=0
+        )
+        for i in range(2):
+            to = pl.multiple_of((2 * double + i) * half, 16)
+            own = h2[0, pl.ds(to, half), :].astype(F32)
+            out[0, pl.ds(to, half), :] = (own + dot(sel[i], sides)).astype(BF)
+
+    sides = jnp.concatenate(
+        [from_left[0, 2 * plan.pairs * hop:], from_right[0, 2 * plan.pairs * hop:]], axis=0
+    )
+    own = h2[0, plan.mid_rows:].astype(F32)
+    out[0, plan.mid_rows:] = (own + dot(edge_sel[...], sides)).astype(BF)
+
+
+def linear_kernel(plan, w_own, w_far, bias, own, far, out):
+    ch = plan.ch
+    wide = w_own.shape[0] // ch
+    for xp in range(own.shape[1] // 2):
+        for g in range(plan.ny // wide):
+            def tile(ref):
+                sides = [
+                    ref[:, 2 * xp + i, g * wide:(g + 1) * wide, :].reshape(ch * wide, LANES)
+                    for i in range(2)
+                ]
+                return jnp.concatenate(sides, axis=1)
+
+            total = dot(w_own[...], tile(own)) + dot(w_far[...], tile(far)) + bias[...]
+            total = total.astype(BF)
+            for i in range(2):
+                out[:, 2 * xp + i, g * wide:(g + 1) * wide, :] = total[
+                    :, i * LANES:(i + 1) * LANES
+                ].reshape(ch, wide, LANES)
+
+
+def mix_kernel(plan, fx, weights, pencils, out, coeffs):
+    step = pl.program_id(0)
+    ch, rows = plan.ch, weights.shape[2]
+
+    @pl.when(step == 0)
+    def _():
+        @pl.loop(0, ch)
+        def _(c):
+            column = jnp.concatenate([pencils[d, c] for d in range(plan.slabs)], axis=0)
+            coeffs[c] = dot(fx[...], column).astype(BF).astype(F32)
+
+    start = pl.multiple_of(step * rows, rows)
+
+    @pl.loop(0, plan.outs)
+    def _(o):
+        total = weights[0, o].astype(F32) * coeffs[0, pl.ds(start, rows), :]
+        for c in range(1, ch):
+            total = total + weights[c, o].astype(F32) * coeffs[c, pl.ds(start, rows), :]
+        out[o] = total.astype(BF)
+
+
+def sum_kernel(plan, mine, got, out):
+    out[...] = (mine[...].astype(F32) + got[...].astype(F32)).astype(BF)
+
+
+def back_x_kernel(plan, gx, mixed, out):
+    done = dot(gx[...], mixed[0]).astype(BF)
+    for k in range(plan.slabs):
+        out[k, 0] = done[k * plan.planes:(k + 1) * plan.planes]
+
+
+def final_kernel(plan, meta, gz2, gzp2, gx3, gy, interp, lin, h1, h2, modes0, owns, out, scr, wide,
+                 place):
+    nb, slabs, planes, modes, half = plan.blocks, plan.slabs, plan.planes, plan.modes, plan.half
+    depth = plan.depth
+    coarse = meta[3 * nb + 1] == 0
+    step = pl.program_id(0)
+
+    @pl.when(step == 0)
+    def _():
+        info = listing(meta, plan)
+        row, col = row_col(plan.ny, modes)
+        block = steps_of(row, plan.rows, nb)
+        wide[:, 0:modes] = gy[...]
+        for which, base in ((1, 1), (2, 0), (3, 2)):
+            fed = by_block(block, [meta[base * nb + b] for b in range(nb)]) == info["slab"]
+            wide[:, which * modes:(which + 1) * modes] = jnp.where(
+                fed, gy[...].astype(F32), 0.0
+            ).astype(BF)
+        row, col = row_col(plan.ny, plan.ny)
+        block = steps_of(row, plan.rows, nb)
+        slot = steps_of(col, plan.rows, nb)
+        same = row - block * plan.rows == col - slot * plan.rows
+        listed = by_block(block, info["listed"]) == 1
+        place[...] = chosen(same & listed & (by_block(block, info["place"]) == slot)).astype(BF)
+
+    for d in range(slabs):
+        left = jnp.concatenate(
+            [owns[d, 0, :, jp * LANES:(jp + 1) * LANES] for jp in range(plan.group // 2)], axis=0
+        )
+        done = dot(left, gz2[...])
+        for jp in range(plan.group // 2):
+            for i in range(2):
+                m = d * plan.group + 2 * jp + i
+                scr[pl.ds(m, planes, stride=depth), :] = done[
+                    jp * planes:(jp + 1) * planes, i * LANES:(i + 1) * LANES
+                ]
+
+    @pl.when(coarse)
+    def _():
+        for d in range(slabs):
+            beside = dot(gx3[...], modes0[d, 0]).astype(BF)
+            left = jnp.concatenate(
+                [beside[:, jp * LANES:(jp + 1) * LANES] for jp in range(plan.group // 2)], axis=0
+            )
+            done = dot(left, gzp2[...])
+            for jp in range(plan.group // 2):
+                for which in range(3):
+                    at = (jp * 3 + which) * planes
+                    for i in range(2):
+                        m = (which + 1) * modes + d * plan.group + 2 * jp + i
+                        scr[pl.ds(m, planes, stride=depth), :] = done[
+                            at:at + planes, i * LANES:(i + 1) * LANES
+                        ]
+
+    def emit(xp, total):
+        for i in range(2):
+            for r in range(0, plan.ny, 16):
+                v = total[r:r + 16, i * LANES:(i + 1) * LANES] + lin[
+                    0, 2 * xp + i, r:r + 16, :
+                ].astype(F32)
+                out[0, 2 * xp + i, r:r + 16, :] = gelu(v).astype(BF)
+
+    def spread(xp, count):
+        sides = []
+        for i in range(2):
+            at = pl.multiple_of((2 * xp + i) * depth, 8)
+            sides.append(scr[pl.ds(at, count), :])
+        return jnp.concatenate(sides, axis=1).astype(BF)
+
+    @pl.when(coarse)
+    def _():
+        @pl.loop(0, plan.pairs, unroll=2)
+        def _(xp):
+            emit(xp, dot(wide[...], spread(xp, 4 * modes)))
+
+    @pl.when(jnp.logical_not(coarse))
+    def _():
+        c2 = lax.rem(step, 2)
+
+        @pl.loop(0, plan.pairs, unroll=2)
+        def _(xp):
+            at = pl.multiple_of((c2 * plan.pairs + xp) * half, 16)
+            table = interp[c2 * plan.pairs + xp]
+            parts = []
+            for ref in (h1, h2):
+                packed = jnp.concatenate(
+                    [ref[0, pl.ds(at, half), :], ref[0, plan.mid_rows:]], axis=1
+                )
+                parts.append(dot(packed, table).astype(BF))
+            fed = dot(place[...], jnp.concatenate(parts, axis=0))
+            emit(xp, fed + dot(gy[...], spread(xp, modes)))
+
+
+def whole(shape):
+    return pl.BlockSpec(shape, lambda *_: (0,) * len(shape))
+
+
+SCALARS = pl.BlockSpec(memory_space=pltpu.SMEM)
+
+
+def edge_select(plan):
+    lo, mid = plan.nz // 4, plan.nz // 2
+    sel = np.zeros((2, plan.planes, plan.nz, LANES), np.float32)
+    for c2 in range(2):
+        for x in range(plan.planes):
+            at = c2 * 2 * plan.planes + 2 * x
+            sel[c2, x, lo - 1, at] = 1.0
+            sel[c2, x, lo + mid, at + 1] = 1.0
+    return sel
+
+
+def call(kernel, plan, grid, in_specs, out_specs, out_shape, scratch, cost, args, after=(),
+         onto=None):
+    count = len(args)
+    aliases = {}
+    if onto is not None:
+        aliases = {count: 0}
+        after = (onto,) + tuple(after)
+
+    def run(*refs):
+        kernel(plan, *refs[:count], *refs[count + len(after):])
+
+    flops, traffic, special = cost
+    return pl.pallas_call(
+        run,
+        grid=grid,
+        in_specs=in_specs + [pl.BlockSpec(memory_space=pl.ANY)] * len(after),
+        out_specs=out_specs,
+        out_shape=out_shape,
+        scratch_shapes=scratch,
+        input_output_aliases=aliases,
+        compiler_params=pltpu.CompilerParams(vmem_limit_bytes=56 * 2**20),
+        cost_estimate=pl.CostEstimate(
+            flops=1000, bytes_accessed=1000, transcendentals=0
+        ),
+    )(*args, *after)
+
+
+def gate(value, after):
+    anywhere = pl.BlockSpec(memory_space=pl.ANY)
+    return pl.pallas_call(
+        lambda *refs: None,
+        in_specs=[anywhere] * (1 + len(after)),
+        out_specs=anywhere,
+        out_shape=jax.ShapeDtypeStruct(value.shape, value.dtype),
+        input_output_aliases={0: 0},
+    )(value, *after)
+
+
+def run_forward(plan, fy, fz2, field, after=()):
+    shape = (plan.slabs, plan.ch, plan.planes, plan.q)
+    return call(
+        forward_kernel, plan, (plan.ch,),
+        [whole(fy.shape), whole(fz2.shape), plan.chan_spec()],
+        pl.BlockSpec((plan.slabs, 1, plan.planes, plan.q), lambda c: (0, c, 0, 0)),
+        jax.ShapeDtypeStruct(shape, BF),
+        [pltpu.VMEM((plan.modes * plan.step, LANES), F32)],
+        (10**9, field.size * 2, 0), (fy, fz2, field), after,
+    )
+
+
+def run_pack(plan, meta, esel, field, group, near, after=()):
+    start, count = group
+    full = jax.ShapeDtypeStruct((count, plan.pack_rows, LANES), BF)
+    part = jax.ShapeDtypeStruct((count, plan.nb_rows, LANES), BF)
+    shapes = [full, part, part] if near else [full]
+    rows = plan.half + 2 * plan.edge_rows if near else plan.half
+    return call(
+        pack_rest_kernel if near else pack_first_kernel, plan, (count,),
+        [SCALARS, whole(esel.shape),
+         pl.BlockSpec((2,) + field.shape[1:], lambda c: (c + start, 0, 0, 0))],
+        [pl.BlockSpec((1,) + shape.shape[1:], lambda c: (c, 0, 0)) for shape in shapes], shapes,
+        [pltpu.VMEM((rows, plan.ny), BF)],
+        (10**9, field.size * 3, 0), (meta, esel, field), after,
+    )
+
+
+def run_assemble(plan, meta, second, from_left, from_right, after=()):
+    pack_spec = pl.BlockSpec((1, plan.pack_rows, LANES), lambda c: (c, 0, 0))
+    near_spec = pl.BlockSpec((1, plan.nb_rows, LANES), lambda c: (c, 0, 0))
+    return call(
+        assemble_kernel, plan, (second.shape[0],),
+        [SCALARS, pack_spec, near_spec, near_spec], pack_spec,
+        jax.ShapeDtypeStruct(second.shape, BF),
+        [pltpu.VMEM((2, plan.half, 4 * plan.hop), BF),
+         pltpu.VMEM((plan.half, 2 * plan.edge_rows), BF)],
+        (10**9, second.size * 6, 0), (meta, second, from_left, from_right), after,
+    )
+
+
+def run_linear(plan, w_own, w_far, bias_rows, field, far_field, after=()):
+    per = 4
+    spec = pl.BlockSpec((plan.ch, per) + field.shape[2:], lambda x: (0, x, 0, 0))
+    return call(
+        linear_kernel, plan, (plan.planes // per,),
+        [whole(w_own.shape), whole(w_far.shape), whole(bias_rows.shape), spec, spec],
+        spec, jax.ShapeDtypeStruct(field.shape, BF), [],
+        (2 * 10**10, field.size * 6, 0), (w_own, w_far, bias_rows, field, far_field), after,
+    )
+
+
+def run_mix(plan, fx, weights, pencils, after=()):
+    rows = 16
+    return call(
+        mix_kernel, plan, (plan.modes // rows,),
+        [whole(fx.shape),
+         pl.BlockSpec((plan.ch, plan.outs, rows, plan.q), lambda n: (0, 0, n, 0)),
+         whole(pencils.shape)],
+        pl.BlockSpec((plan.outs, rows, plan.q), lambda n: (0, n, 0)),
+        jax.ShapeDtypeStruct((plan.outs, plan.modes, plan.q), BF),
+        [pltpu.VMEM((plan.ch, plan.modes, plan.q), F32)],
+        (10**9, weights.size * 2, 0), (fx, weights, pencils), after,
+    )
+
+
+def run_sum(plan, mine, got, after=()):
+    return call(
+        sum_kernel, plan, (1,), [whole(mine.shape), whole(mine.shape)], whole(mine.shape),
+        jax.ShapeDtypeStruct(mine.shape, BF), [], (1, 1, 0), (mine, got), after,
+    )
+
+
+def run_back_x(plan, gx, mixed, after=()):
+    return call(
+        back_x_kernel, plan, (plan.ch,),
+        [whole(gx.shape), pl.BlockSpec((1, plan.modes, plan.q), lambda c: (c, 0, 0))],
+        pl.BlockSpec((plan.slabs, 1, plan.planes, plan.q), lambda c: (0, c, 0, 0)),
+        jax.ShapeDtypeStruct((plan.slabs, plan.ch, plan.planes, plan.q), BF), [],
+        (10**9, mixed.size * 10, 0), (gx, mixed), after,
+    )
+
+
+def run_final(plan, meta, gz2, gzp2, gx3, gy, interp, lin, first, second, fine_modes, owned, group,
+              onto=None, after=()):
+    start, count = group
+    at = 2 * start
+    chan_spec = pl.BlockSpec((1,) + lin.shape[1:], lambda c: (c + at, 0, 0, 0))
+    pair_spec = pl.BlockSpec((1, plan.pack_rows, LANES), lambda c: (c // 2, 0, 0))
+    return call(
+        final_kernel, plan, (2 * count,),
+        [SCALARS, whole(gz2.shape), whole(gzp2.shape), whole(gx3.shape), whole(gy.shape),
+         whole(interp.shape), chan_spec, pair_spec, pair_spec,
+         pl.BlockSpec((plan.slabs, 1, plan.modes, plan.q), lambda c: (0, c, 0, 0)),
+         pl.BlockSpec((plan.slabs, 1, plan.planes, plan.q), lambda c: (0, c + at, 0, 0))],
+        chan_spec, jax.ShapeDtypeStruct(lin.shape, BF),
+        [pltpu.VMEM((plan.planes * plan.depth, LANES), F32),
+         pltpu.VMEM((plan.ny, 4 * plan.modes), BF),
+         pltpu.VMEM((plan.ny, plan.ny), BF)],
+        (10**10, lin.size * 6, lin.size),
+        (meta, gz2, gzp2, gx3, gy, interp, lin, first, second, fine_modes, owned), after, onto,
+    )
+
+
+def interp_tables(plan):
+    fine = host_interp(plan.nz).T
+    lo, mid = plan.nz // 4, plan.nz // 2
+    table = np.zeros((2, plan.pairs, 2 * LANES, 2 * plan.nz), np.float32)
+    for c2 in range(2):
+        for x in range(plan.planes):
+            side = x % 2
+            spot = table[c2, x // 2, :, side * plan.nz:(side + 1) * plan.nz]
+            spot[side * mid:(side + 1) * mid] = fine[lo:lo + mid]
+            at = LANES + c2 * 2 * plan.planes + 2 * x
+            spot[at] = fine[lo - 1]
+            spot[at + 1] = fine[lo + mid]
+    return table.reshape(2 * plan.pairs, 2 * LANES, 2 * plan.nz).astype(ml_dtypes.bfloat16)
+
+
+def pointwise(plan, lin_local, bias_local, ch_id, wide=16):
+    size = plan.ch * wide
+    eye = jnp.eye(wide, dtype=F32)
+    kron = jnp.einsum("io,ab->oaib", lin_local.astype(F32), eye).astype(BF)
+    kron = kron.reshape(size, 2, size).transpose(1, 0, 2)
+    w_own = lax.dynamic_index_in_dim(kron, ch_id, 0, keepdims=False)
+    w_far = lax.dynamic_index_in_dim(kron, 1 - ch_id, 0, keepdims=False)
+    bias_rows = jnp.repeat(bias_local.astype(F32), wide)[:, None]
+    return w_own, w_far, jnp.broadcast_to(bias_rows, (size, 2 * LANES))
+
+
+def fast_body(plan, field, mode_local, lin_local, bias_local, own_row):
+    slabs, planes, ch, modes = plan.slabs, plan.planes, plan.ch, plan.modes
+    slab_id = lax.axis_index("slab")
+    pool_id = lax.axis_index("pool")
+    ch_id = lax.axis_index("ch")
+    fwd_x, inv_x = host_tables(plan.nx, modes)
+    fwd_y, inv_y = host_tables(plan.ny, modes)
+    fwd_z, inv_z = host_tables(plan.nz, modes)
+    esel = edge_select(plan).reshape(2 * plan.pairs, 2 * plan.nz, LANES)
+    esel = esel.astype(ml_dtypes.bfloat16)
+
+    above = shifted(own_row, "slab", 1)
+    below = shifted(own_row, "slab", -1)
+    far_field = swapped(field, "ch", 0)
+    meta = jnp.concatenate([
+        own_row,
+        jnp.where(slab_id > 0, above, -1),
+        jnp.where(slab_id < slabs - 1, below, -1),
+        jnp.stack([slab_id, pool_id]).astype(jnp.int32),
+    ])
+
+    sent = gate(run_forward(plan, fwd_y, two_of(fwd_z.T), field), (meta,))
+    pencils = lax.all_to_all(sent, "slab", split_axis=0, concat_axis=0, tiled=True)
+
+    both = ("pool", "slab")
+    firsts, packs, last = [], [], sent
+    for group in plan.groups:
+        last = run_pack(plan, meta, esel, field, group, False, (last,))[0]
+        firsts.append(lax.ppermute(last, "pool", [(0, 1)]))
+        last, to_right, to_left = run_pack(plan, meta, esel, field, group, True, (last,))
+        packs.append((
+            last,
+            lax.ppermute(to_right, both, [(i, i + 1) for i in range(slabs - 1)]),
+            lax.ppermute(to_left, both, [(i + 1, i) for i in range(slabs - 1)]),
+        ))
+
+    partial = run_mix(plan, fwd_x, mode_local, pencils, (last,))
+    halves = partial.reshape(2, ch, modes, plan.q)
+    mine = lax.dynamic_index_in_dim(halves, ch_id, 0, keepdims=False)
+    theirs = lax.dynamic_index_in_dim(halves, 1 - ch_id, 0, keepdims=False)
+    mixed = run_sum(plan, mine, swapped(theirs, "ch", 0), (firsts[0],))
+
+    back = run_back_x(plan, inv_x, mixed)
+    owned = lax.all_to_all(back, "slab", split_axis=0, concat_axis=0, tiled=True)
+
+    w_own, w_far, bias_rows = pointwise(plan, lin_local, bias_local, ch_id)
+    lin = run_linear(plan, w_own, w_far, bias_rows, field, far_field, (back,))
+
+    lead = 2 * plan.groups[0][1]
+    rest = ch - lead
+    hop = lax.ppermute(mixed[:lead], "pool", [(1, 0)])
+    here = jnp.where(pool_id == 0, hop, mixed[ch - lead:])
+    here = gate(here, (back,) + packs[0][1:])
+    here = lax.all_gather(here, "slab", axis=0, tiled=False)
+    seconds, last = [], lin
+    for second, from_left, from_right in packs:
+        last = run_assemble(plan, meta, second, from_left, from_right, (last, firsts[-1]))
+        seconds.append(lax.ppermute(last, "pool", [(0, 1)]))
+    over = gate(here[:, lead - rest:], (last,))
+    gathered = [here, lax.ppermute(over, "pool", [(1, 0)])]
+
+    to_coarse = 0.5 * host_interp(plan.nz)
+    gzp = (inv_z.T.astype(np.float32) @ to_coarse).astype(ml_dtypes.bfloat16)
+    padded = np.pad(inv_x.reshape(slabs, planes, modes), ((1, 1), (0, 0), (0, 0)))
+    gx3 = lax.dynamic_slice_in_dim(jnp.asarray(padded), slab_id, 3, 0)
+    gx3 = gx3.reshape(3 * planes, modes)
+    out = None
+    for group, first_in, second, modes_in in zip(plan.groups, firsts, seconds, gathered):
+        out = run_final(plan, meta, two_of(inv_z.T), two_of(gzp), gx3, inv_y, interp_tables(plan),
+                        lin, first_in, second, modes_in, owned, group, out)
+    return out
+
+
+def plain_body(field, mode_local, lin_local, bias_local, own_row):
+    bias_local = bias_local.astype(jnp.float32)
     own_ch, planes, y_cells, z_cells = field.shape
     modes = mode_local.shape[2]
     x_cells = planes * lax.axis_size("slab")
@@ -124,8 +826,15 @@
         + bias_local[:, None, None, None]
         + coupling.reshape(own_ch, planes, y_cells, z_cells)
     )
-    field = jax.nn.gelu(total, approximate=False).astype(jnp.bfloat16)
-    return field[None]
+    return jax.nn.gelu(total, approximate=False).astype(jnp.bfloat16)
+
+
+def body(fields, mode_weights, lin_weights, bias, source):
+    args = (fields[0], mode_weights[0], lin_weights[0], bias[0], source[0])
+    plan = Plan(args[0], args[1], args[4], lax.axis_size("slab"))
+    if plan.fits():
+        return fast_body(plan, *args)[None]
+    return plain_body(*args)[None]
 
 
 def solution(mesh):

time: 1190 us -> 354 us (0.30)
  waiting for transfers between devices: 662 us -> 75.2 us
  Pallas kernels: 0 us -> 178 us
  matrix products: 173 us -> 0 us
  local copies, waits for them, and re-layouts: 140 us -> 16 us
  other arithmetic: 102 us -> 1.98 us
  blocking collectives: 63.9 us -> 0 us
  starting transfers between devices: 26.1 us -> 68 us
    ppermute x1 -> x2, waiting for transfers between devices: 385 us -> 0.01 us  [swapped(): return lax.ppermute(value, axis, pairs)]
    ppermute x6 -> x2, waiting for transfers between devices: 178 us -> 0.01 us  [shifted(): lax.ppermute(value, axis, [(source, source + steps) for source in range(l...]
    pallas_call x0 -> x16, Pallas kernels: none -> 178 us  [the longest x13 178 us: call(): pl.pallas_call(run, grid=grid, in_specs=in_specs + [pl.BlockSpec(memory_s...]
    dot_general x10 -> x0, matrix products: 173 us -> none  [the longest x2 48.5 us: body(): jnp.einsum('hb,cxhr->cxbr', placing, arrived, preferred_element_type=jnp....]
    broadcast_in_dim x1 -> x0, other arithmetic: 91.5 us -> none  [body(): return field[None]]
    reshape x4 -> x1, local copies, waits for them, and re-layouts: 91.5 us -> 2.34 us  [pointwise(): kron = kron.reshape(size, 2, size).transpose(1, 0, 2)]
    all_to_all x1 -> x2, waiting for transfers between devices: 89.6 us -> 14 us  [the longest x1 14 us: fast_body(): lax.all_to_all(sent, 'slab', split_axis=0, concat_axis=0, tiled=True)]
    all_to_all x1 -> x0, blocking collectives: 63.9 us -> none  [body(): lax.all_to_all(along_z, 'slab', split_axis=2, concat_axis=1, tiled=True)]
  transfers between devices with their start and end apart: 10 -> 17, of which waited for: 5 -> 4; matrix products, arithmetic and copies ran while one was open for 16% -> 4% of each run, Pallas kernels for 0% -> 42%
where the time goes in v1:
time: 354 us; the launch traced here: 352 us
  Pallas kernels  178 us (50%)
  waiting for transfers between devices  75.2 us (21%)
  starting transfers between devices  68 us (19%)
  local copies, waits for them, and re-layouts  16 us (5%)
  between operations  13.6 us (4%)
    pallas_call x13, Pallas kernels, call(): pl.pallas_call(run, grid=grid, in_specs=in_specs + [pl.BlockSpec(memory_s...  178 us
    all_gather x1, waiting for transfers between devices, fast_body(): here = lax.all_gather(here, 'slab', axis=0, tiled=False)  36.3 us
    ppermute x1, starting transfers between devices, fast_body(): gathered = [here, lax.ppermute(over, 'pool', [(1, 0)])]  35.1 us
    ppermute x2, waiting for transfers between devices, fast_body(): firsts.append(lax.ppermute(last, 'pool', [(0, 1)]))  24.8 us
    all_to_all x1, waiting for transfers between devices, fast_body(): lax.all_to_all(sent, 'slab', split_axis=0, concat_axis=0, tiled=True)  14 us
    all_to_all x1, starting transfers between devices, fast_body(): lax.all_to_all(back, 'slab', split_axis=0, concat_axis=0, tiled=True)  7.37 us
  transfers between devices with their start and end apart: 17, of which 4 were waited for; matrix products, arithmetic and copies ran while one was open for 4% of the time, Pallas kernels for 42%

profile of v1, /device:TPU:18, one launch (start us, length us, event | category | flops | bytes accessed | tf_op | source)
XLA Modules:
  0.0 352.3 jit_solution(10181032270285287753)
XLA Ops:
  6.5 3.4 collective-permute-start.1
  10.0 2.5 collective-permute-start
  12.5 13.6 %shard_map.172.refs_0_ = bf16[8,10,32,512]{3,2,1,0:T(8,128)(2,1)} custom-call(bf16[64,224]{1,0:T(8,128)(2,1)} %constant.57.clone.refs_0_, bf16[256,128]{1,0:T(8,128)(2,1)} %constant.58.clone.refs_1_, bf16[10,32,224,128]{3,2,1,0:T(8,128)(2,1)} %bitcast.26), custom_call_target="tpu_custom_call" | custom-call | flops 1000 | bytes 1000 | tf_op jit(solution)/shard_map/pallas_call | solution.py:518
  26.7 6.0 %all-to-all-start = ((bf16[8,10,32,512]{3,2,1,0:T(8,128)(2,1)}), bf16[8,10,32,512]{3,2,1,0:T(8,128)(2,1)}, u32[]{:S(2)}, u32[]{:S(2)}) async-start(bf16[8,10,32,512]{3,2,1,0:T(8,128)(2,1)} %shard_map.173.refs_3_), calls=%async_computation | async-start | bytes 5242880 | tf_op jit(solution)/shard_map/all_to_all | solution.py:696
  32.8 10.1 %shard_map.174.refs_3_ = bf16[3,3696,128]{2,1,0:T(8,128)(2,1)} custom-call(s32[26]{0:T(128)} %concatenate.3.refs_1_.refs_0_, bf16[32,256,128]{2,1,0:T(8,128)(2,1)} %constant.59.clone.refs_1_, bf16[10,32,224,128]{3,2,1,0:T(8,128)(2,1)} %bitcast.27, bf16[8,10,32,512]{3,2,1,0:T(8,128)(2,1)} %shard_map.173.refs_3_), custom_call_target="tpu_custom_call" | custom-call | flops 1000 | bytes 1000 | tf_op jit(solution)/shard_map/pallas_call | solution.py:518
  44.1 11.2 %shard_map.175 = (bf16[3,3696,128]{2,1,0:T(8,128)(2,1)}, bf16[3,1856,128]{2,1,0:T(8,128)(2,1)}, bf16[3,1856,128]{2,1,0:T(8,128)(2,1)}) custom-call(s32[26]{0:T(128)} %concatenate.3.refs_1_.refs_0_, bf16[32,256,128]{2,1,0:T(8,128)(2,1)} %constant.59.clone.refs_1_, bf16[10,32,224,128]{3,2,1,0:T(8,128)(2,1)} %bitcast.28, bf16[3,3696,128]{2,1,0:T(8,128)(2,1)} %shard_map.174.refs_3_), custom_call_target="tpu_custom_call" | custom-call | flops 1000 | bytes 1000 | tf_op jit(solution)/shard_map/pallas_call | solution.py:518
  55.3 1.8 collective-permute-start.8
  57.0 7.8 %shard_map.176.refs_3_ = bf16[2,3696,128]{2,1,0:T(8,128)(2,1)} custom-call(s32[26]{0:T(128)} %concatenate.3.refs_1_.refs_0_, bf16[32,256,128]{2,1,0:T(8,128)(2,1)} %constant.59.clone.refs_1_, bf16[10,32,224,128]{3,2,1,0:T(8,128)(2,1)} %bitcast.29, bf16[3,3696,128]{2,1,0:T(8,128)(2,1)} %get-tuple-element.11.refs_3_.refs_1_), custom_call_target="tpu_custom_call" | custom-call | flops 1000 | bytes 1000 | tf_op jit(solution)/shard_map/pallas_call | solution.py:518
  64.8 1.8 collective-permute-start.9
  66.6 8.5 %shard_map.177 = (bf16[2,3696,128]{2,1,0:T(8,128)(2,1)}, bf16[2,1856,128]{2,1,0:T(8,128)(2,1)}, bf16[2,1856,128]{2,1,0:T(8,128)(2,1)}) custom-call(s32[26]{0:T(128)} %concatenate.3.refs_1_.refs_0_, bf16[32,256,128]{2,1,0:T(8,128)(2,1)} %constant.59.clone.refs_1_, bf16[10,32,224,128]{3,2,1,0:T(8,128)(2,1)} %bitcast.30, bf16[2,3696,128]{2,1,0:T(8,128)(2,1)} %shard_map.176.refs_3_), custom_call_target="tpu_custom_call" | custom-call | flops 1000 | bytes 1000 | tf_op jit(solution)/shard_map/pallas_call | solution.py:518
  75.1 14.0 %all-to-all-done.refs_2_ = bf16[8,10,32,512]{3,2,1,0:T(8,128)(2,1)} async-done(((bf16[8,10,32,512]{3,2,1,0:T(8,128)(2,1)}), bf16[8,10,32,512]{3,2,1,0:T(8,128)(2,1)}, u32[]{:S(2)}, u32[]{:S(2)}) %all-to-all-start) | async-done | bytes 2621472 | tf_op jit(solution)/shard_map/all_to_all | solution.py:696
  89.1 10.2 %shard_map.178 = bf16[20,64,512]{2,1,0:T(8,128)(2,1)} custom-call(bf16[64,256]{1,0:T(8,128)(2,1)} %constant.60.clone.refs_0_, bf16[10,20,64,512]{3,2,1,0:T(8,128)(2,1)} %bitcast.32, bf16[8,10,32,512]{3,2,1,0:T(8,128)(2,1)} %all-to-all-done.refs_2_, bf16[2,3696,128]{2,1,0:T(8,128)(2,1)} %get-tuple-element.12.refs_3_.refs_1_), custom_call_target="tpu_custom_call" | custom-call | flops 1000 | bytes 1000 | tf_op jit(solution)/shard_map/pallas_call | solution.py:518
  99.2 2.2 dynamic-slice_bitcast_fusion
  101.5 6.3 %collective-permute-done.4.refs_2_.refs_7_ = bf16[3,3696,128]{2,1,0:T(8,128)(2,1)S(1)} collective-permute-done((bf16[3,3696,128]{2,1,0:T(8,128)(2,1)}, bf16[3,3696,128]{2,1,0:T(8,128)(2,1)S(1)}, u32[]{:S(2)}, u32[]{:S(2)}) %collective-permute-start.4) | collective-permute-done | bytes 2838560 | tf_op jit(solution)/shard_map/ppermute | solution.py:702
  107.7 1.6 copy-done.1
  109.5 2.3 shard_map.179.refs_1_
  112.9 1.6 collective-permute-start.11
  114.5 7.2 %shard_map.180.refs_5_.refs_1_ = bf16[8,10,32,512]{3,2,1,0:T(8,128)(2,1)} custom-call(bf16[256,64]{1,0:T(8,128)(2,1)} %constant.61.clone.refs_0_, bf16[10,64,512]{2,1,0:T(8,128)(2,1)} %shard_map.179.refs_1_), custom_call_target="tpu_custom_call" | custom-call | flops 1000 | bytes 1000 | tf_op jit(solution)/shard_map/pallas_call | solution.py:518
  123.8 7.4 %all-to-all-start.1 = ((bf16[8,10,32,512]{3,2,1,0:T(8,128)(2,1)}), bf16[8,10,32,512]{3,2,1,0:T(8,128)(2,1)S(1)}, u32[]{:S(2)}, u32[]{:S(2)}) async-start(bf16[8,10,32,512]{3,2,1,0:T(8,128)(2,1)} %shard_map.180.refs_5_.refs_1_), calls=%async_computation.1 | async-start | bytes 5242880 | tf_op jit(solution)/shard_map/all_to_all | solution.py:717
  132.5 2.3 reshape.22
  135.3 1.6 collective-permute-start.6
  136.9 1.7 collective-permute-start.7
  140.0 22.8 %shard_map.181.refs_4_.refs_6_ = bf16[10,32,224,128]{3,2,1,0:T(8,128)(2,1)} custom-call(bf16[160,160]{1,0:T(8,128)(2,1)} %get-tuple-element.22.refs_0_, bf16[160,160]{1,0:T(8,128)(2,1)} %get-tuple-element.21.refs_1_, f32[160,256]{1,0:T(8,128)} %broadcast_in_dim.21.refs_2_, bf16[10,32,224,128]{3,2,1,0:T(8,128)(2,1)} %bitcast.31, ...), custom_call_target="tpu_custom_call" | custom-call | flops 1000 | bytes 1000 | tf_op jit(solution)/shard_map/pallas_call | solution.py:518
  162.8 18.6 %collective-permute-done.5.refs_5_.refs_7_ = bf16[2,3696,128]{2,1,0:T(8,128)(2,1)} collective-permute-done((bf16[2,3696,128]{2,1,0:T(8,128)(2,1)}, bf16[2,3696,128]{2,1,0:T(8,128)(2,1)}, u32[]{:S(2)}, u32[]{:S(2)}) %collective-permute-start.5) | collective-permute-done | bytes 1892384 | tf_op jit(solution)/shard_map/ppermute | solution.py:702
  181.3 7.6 %shard_map.182.refs_4_ = bf16[3,3696,128]{2,1,0:T(8,128)(2,1)} custom-call(s32[26]{0:T(128)} %concatenate.3.refs_1_.refs_0_, bf16[3,3696,128]{2,1,0:T(8,128)(2,1)} %get-tuple-element.11.refs_3_.refs_1_, bf16[3,1856,128]{2,1,0:T(8,128)(2,1)} %collective-permute-done.8.refs_2_, bf16[3,1856,128]{2,1,0:T(8,128)(2,1)} %collective-permute-done.9.refs_3_, ...), custom_call_target="tpu_custom_call" | custom-call | flops 1000 | bytes 1000 | tf_op jit(solution)/shard_map/pallas_call | solution.py:518
  190.2 36.3 %all-gather.3.cloned.1.call-done = bf16[48,64,512]{2,1,0:T(8,128)(2,1)} async-done(((bf16[6,64,512]{2,1,0:T(8,128)(2,1)}), bf16[48,64,512]{2,1,0:T(8,128)(2,1)}) %all-gather.3.cloned.1.call-update) | async-done | bytes 3145744 | tf_op jit(solution)/shard_map/all_gather | solution.py:727
  226.6 3.1 slice.14.refs_0_
  229.7 5.9 %shard_map.183.refs_1_ = bf16[2,3696,128]{2,1,0:T(8,128)(2,1)} custom-call(s32[26]{0:T(128)} %concatenate.3.refs_1_.refs_0_, bf16[2,3696,128]{2,1,0:T(8,128)(2,1)} %get-tuple-element.12.refs_3_.refs_1_, bf16[2,1856,128]{2,1,0:T(8,128)(2,1)} %collective-permute-done.6.refs_2_, bf16[2,1856,128]{2,1,0:T(8,128)(2,1)} %collective-permute-done.7.refs_3_, ...), custom_call_target="tpu_custom_call" | custom-call | flops 1000 | bytes 1000 | tf_op jit(solution)/shard_map/pallas_call | solution.py:518
  235.6 35.1 %collective-permute-start.12 = (bf16[8,4,64,512]{3,2,1,0:T(8,128)(2,1)}, bf16[8,4,64,512]{3,2,1,0:T(8,128)(2,1)}, u32[]{:S(2)}, u32[]{:S(2)}) collective-permute-start(bf16[8,4,64,512]{3,2,1,0:T(8,128)(2,1)} %shard_map.185), channel_id=1, source_target_pairs={{16,0},{17,1},{18,2},{19,3},{20,4},{21,5},{22,6},{23,7},{24,8},{25... | collective-permute-start | bytes 6291464 | tf_op jit(solution)/shard_map/ppermute | solution.py:733
  273.4 1.5 copy-done
  274.9 41.3 %shard_map.186.refs_11_ = bf16[10,32,224,128]{3,2,1,0:T(8,128)(2,1)} custom-call(s32[26]{0:T(128)} %concatenate.3.refs_1_.refs_0_, bf16[128,256]{1,0:T(8,128)(2,1)} %constant.63.clone.refs_1_, bf16[128,256]{1,0:T(8,128)(2,1)} %constant.64.clone.refs_2_, bf16[96,64]{1,0:T(8,128)(2,1)} %bitcast.36, bf16[224,64]{1,0:T(8,128)(2,1)} %constant.65.clone.refs_4_, ...), custom_call_target="tpu_custom_call" | custom-call | flops 1000 | bytes 1000 | tf_op jit(solution)/shard_map/pallas_call | solution.py:518
  316.2 29.3 %shard_map.187 = bf16[10,32,224,128]{3,2,1,0:T(8,128)(2,1)} custom-call(s32[26]{0:T(128)} %concatenate.3.refs_1_.refs_0_, bf16[128,256]{1,0:T(8,128)(2,1)} %constant.63.clone.refs_1_, bf16[128,256]{1,0:T(8,128)(2,1)} %constant.64.clone.refs_2_, bf16[96,64]{1,0:T(8,128)(2,1)} %bitcast.37, ...), custom_call_target="tpu_custom_call", output_to_operand_aliasing={{}: (11, {})} | custom-call | flops 1000 | bytes 1000 | tf_op jit(solution)/shard_map/pallas_call | solution.py:518
  (51 shorter events, 12.4 us)
Async XLA Ops:
  6.5 132.7 %collective-permute-start.2 = (bf16[10,32,224,128]{3,2,1,0:T(8,128)(2,1)}, bf16[10,32,224,128]{3,2,1,0:T(8,128)(2,1)}, u32[]{:S(2)}, u32[]{:S(2)}) collective-permute-start(bf16[10,32,224,128]{3,2,1,0:T(8,128)(2,1)} %bitcast.25), channel_id=1, source_target_pairs={{0,1},{1,0},{2,3},{3,2},{4,5},{5,4},{6,7},{7,6},{8,9},{9,8},{10,11... | collective-permute-start | bytes 55050248 | tf_op jit(solution)/shard_map/ppermute | solution.py:31
  6.5 19.6 %copy-start.5 = (s32[1,8]{1,0:T(1,128)S(1)}, s32[1,8]{1,0:T(1,128)}, u32[]{:S(2)}) copy-start(s32[1,8]{1,0:T(1,128)} %param.22) | copy-start | bytes 100
  6.5 19.5 %collective-permute-start.1 = (s32[8]{0:T(128)}, s32[8]{0:T(128)S(1)}, u32[]{:S(2)}, u32[]{:S(2)}) collective-permute-start(s32[8]{0:T(128)} %bitcast.38), channel_id=1, source_target_pairs={{2,0},{4,2},{6,4},{8,6},{10,8},{12,10},{14,12},{3,1},{5,3},{7,5},{... | collective-permute-start | bytes 104 | tf_op jit(solution)/shard_map/ppermute | solution.py:25
  10.0 16.1 %collective-permute-start = (s32[8]{0:T(128)}, s32[8]{0:T(128)S(1)}, u32[]{:S(2)}, u32[]{:S(2)}) collective-permute-start(s32[8]{0:T(128)} %bitcast.39), channel_id=1, source_target_pairs={{0,2},{2,4},{4,6},{6,8},{8,10},{10,12},{12,14},{1,3},{3,5},{5,7},{... | collective-permute-start | bytes 104 | tf_op jit(solution)/shard_map/ppermute | solution.py:25
  26.7 62.4 %all-to-all-start = ((bf16[8,10,32,512]{3,2,1,0:T(8,128)(2,1)}), bf16[8,10,32,512]{3,2,1,0:T(8,128)(2,1)}, u32[]{:S(2)}, u32[]{:S(2)}) async-start(bf16[8,10,32,512]{3,2,1,0:T(8,128)(2,1)} %shard_map.173.refs_3_), calls=%async_computation | async-start | bytes 5242880 | tf_op jit(solution)/shard_map/all_to_all | solution.py:696
  32.8 193.8 %all-gather.3.cloned.1.call-start = ((), (), s32[]{:S(2)}) async-start(), calls=%async_computation.2 | async-start | bytes 3538944 | tf_op jit(solution)/shard_map/all_gather | solution.py:727
  42.8 64.9 %collective-permute-start.4 = (bf16[3,3696,128]{2,1,0:T(8,128)(2,1)}, bf16[3,3696,128]{2,1,0:T(8,128)(2,1)S(1)}, u32[]{:S(2)}, u32[]{:S(2)}) collective-permute-start(bf16[3,3696,128]{2,1,0:T(8,128)(2,1)} %shard_map.174.refs_3_), channel_id=1, source_target_pairs={{0,16},{1,17},{2,18},{3,19},{4,20},{5,21},{6,22},{7,23},{8,24},{9,... | collective-permute-start | bytes 8515592 | tf_op jit(solution)/shard_map/ppermute | solution.py:702
  55.3 67.2 %collective-permute-start.8 = (bf16[3,1856,128]{2,1,0:T(8,128)(2,1)}, bf16[3,1856,128]{2,1,0:T(8,128)(2,1)}, u32[]{:S(2)}, u32[]{:S(2)}) collective-permute-start(bf16[3,1856,128]{2,1,0:T(8,128)(2,1)} %get-tuple-element.15), channel_id=1, source_target_pairs={{0,2},{2,4},{4,6},{6,8},{8,10},{10,12},{12,14},{1,3},{3,5},{5,7},{... | collective-permute-start | bytes 4276232 | tf_op jit(solution)/shard_map/ppermute | solution.py:706
  64.8 57.7 %collective-permute-start.9 = (bf16[3,1856,128]{2,1,0:T(8,128)(2,1)}, bf16[3,1856,128]{2,1,0:T(8,128)(2,1)}, u32[]{:S(2)}, u32[]{:S(2)}) collective-permute-start(bf16[3,1856,128]{2,1,0:T(8,128)(2,1)} %get-tuple-element.16), channel_id=1, source_target_pairs={{2,0},{4,2},{6,4},{8,6},{10,8},{12,10},{14,12},{3,1},{5,3},{7,5},{... | collective-permute-start | bytes 4276232 | tf_op jit(solution)/shard_map/ppermute | solution.py:707
  101.5 6.3 %collective-permute-start.3 = (bf16[10,64,512]{2,1,0:T(8,128)(2,1)S(1)}, bf16[10,64,512]{2,1,0:T(8,128)(2,1)S(1)}, u32[]{:S(2)}, u32[]{:S(2)}) collective-permute-start(bf16[10,64,512]{2,1,0:T(8,128)(2,1)S(1)} %get-tuple-element.17), channel_id=1, source_target_pairs={{0,1},{1,0},{2,3},{3,2},{4,5},{5,4},{6,7},{7,6},{8,9},{9,8},{10,11... | collective-permute-start | bytes 1966088 | tf_op jit(solution)/shard_map/ppermute | solution.py:31
  107.7 1.6 copy-start.1
  107.7 1.8 copy-start.3
  111.8 9.9 %copy-start.2 = (bf16[10,64,512]{2,1,0:T(8,128)(2,1)S(1)}, bf16[10,64,512]{2,1,0:T(8,128)(2,1)}, u32[]{:S(2)}) copy-start(bf16[10,64,512]{2,1,0:T(8,128)(2,1)} %shard_map.179.refs_1_) | copy-start | bytes 1966084
  112.9 8.8 %collective-permute-start.11 = (bf16[6,64,512]{2,1,0:T(8,128)(2,1)S(1)}, bf16[6,64,512]{2,1,0:T(8,128)(2,1)S(1)}, u32[]{:S(2)}, u32[]{:S(2)}) collective-permute-start(bf16[6,64,512]{2,1,0:T(8,128)(2,1)S(1)} %slice.12), channel_id=1, source_target_pairs={{16,0},{17,1},{18,2},{19,3},{20,4},{21,5},{22,6},{23,7},{24,8},{25... | collective-permute-start | bytes 1179656 | tf_op jit(solution)/shard_map/ppermute | solution.py:724
  122.5 8.7 %copy-start.6 = (bf16[1,10]{1,0:T(2,128)(2,1)S(1)}, bf16[1,10]{1,0:T(2,128)(2,1)}, u32[]{:S(2)}) copy-start(bf16[1,10]{1,0:T(2,128)(2,1)} %param.21) | copy-start | bytes 64
  122.5 8.9 %copy-start.4 = (bf16[1,20,10]{1,2,0:T(8,128)(2,1)S(1)}, bf16[1,20,10]{1,2,0:T(8,128)(2,1)}, u32[]{:S(2)}) copy-start(bf16[1,20,10]{1,2,0:T(8,128)(2,1)} %param.20) | copy-start | bytes 1204
  122.5 58.8 %collective-permute-start.5 = (bf16[2,3696,128]{2,1,0:T(8,128)(2,1)}, bf16[2,3696,128]{2,1,0:T(8,128)(2,1)}, u32[]{:S(2)}, u32[]{:S(2)}) collective-permute-start(bf16[2,3696,128]{2,1,0:T(8,128)(2,1)} %shard_map.176.refs_3_), channel_id=1, source_target_pairs={{0,16},{1,17},{2,18},{3,19},{4,20},{5,21},{6,22},{7,23},{8,24},{9,... | collective-permute-start | bytes 5677064 | tf_op jit(solution)/shard_map/ppermute | solution.py:702
  123.8 149.6 %all-to-all-start.1 = ((bf16[8,10,32,512]{3,2,1,0:T(8,128)(2,1)}), bf16[8,10,32,512]{3,2,1,0:T(8,128)(2,1)S(1)}, u32[]{:S(2)}, u32[]{:S(2)}) async-start(bf16[8,10,32,512]{3,2,1,0:T(8,128)(2,1)} %shard_map.180.refs_5_.refs_1_), calls=%async_computation.1 | async-start | bytes 5242880 | tf_op jit(solution)/shard_map/all_to_all | solution.py:717
  135.3 94.4 %collective-permute-start.6 = (bf16[2,1856,128]{2,1,0:T(8,128)(2,1)}, bf16[2,1856,128]{2,1,0:T(8,128)(2,1)}, u32[]{:S(2)}, u32[]{:S(2)}) collective-permute-start(bf16[2,1856,128]{2,1,0:T(8,128)(2,1)} %get-tuple-element.13), channel_id=1, source_target_pairs={{0,2},{2,4},{4,6},{6,8},{8,10},{10,12},{12,14},{1,3},{3,5},{5,7},{... | collective-permute-start | bytes 2850824 | tf_op jit(solution)/shard_map/ppermute | solution.py:706
  136.9 92.8 %collective-permute-start.7 = (bf16[2,1856,128]{2,1,0:T(8,128)(2,1)}, bf16[2,1856,128]{2,1,0:T(8,128)(2,1)}, u32[]{:S(2)}, u32[]{:S(2)}) collective-permute-start(bf16[2,1856,128]{2,1,0:T(8,128)(2,1)} %get-tuple-element.14), channel_id=1, source_target_pairs={{2,0},{4,2},{6,4},{8,6},{10,8},{12,10},{14,12},{3,1},{5,3},{7,5},{... | collective-permute-start | bytes 2850824 | tf_op jit(solution)/shard_map/ppermute | solution.py:707
  188.9 84.4 %collective-permute-start.13 = (bf16[3,3696,128]{2,1,0:T(8,128)(2,1)}, bf16[3,3696,128]{2,1,0:T(8,128)(2,1)}, u32[]{:S(2)}, u32[]{:S(2)}) collective-permute-start(bf16[3,3696,128]{2,1,0:T(8,128)(2,1)} %shard_map.182.refs_4_), channel_id=1, source_target_pairs={{0,16},{1,17},{2,18},{3,19},{4,20},{5,21},{6,22},{7,23},{8,24},{9,... | collective-permute-start | bytes 8515592 | tf_op jit(solution)/shard_map/ppermute | solution.py:731
  235.6 80.6 %collective-permute-start.12 = (bf16[8,4,64,512]{3,2,1,0:T(8,128)(2,1)}, bf16[8,4,64,512]{3,2,1,0:T(8,128)(2,1)}, u32[]{:S(2)}, u32[]{:S(2)}) collective-permute-start(bf16[8,4,64,512]{3,2,1,0:T(8,128)(2,1)} %shard_map.185), channel_id=1, source_target_pairs={{16,0},{17,1},{18,2},{19,3},{20,4},{21,5},{22,6},{23,7},{24,8},{25... | collective-permute-start | bytes 6291464 | tf_op jit(solution)/shard_map/ppermute | solution.py:733
  270.7 45.5 %collective-permute-start.10 = (bf16[2,3696,128]{2,1,0:T(8,128)(2,1)}, bf16[2,3696,128]{2,1,0:T(8,128)(2,1)}, u32[]{:S(2)}, u32[]{:S(2)}) collective-permute-start(bf16[2,3696,128]{2,1,0:T(8,128)(2,1)} %shard_map.183.refs_1_), channel_id=1, source_target_pairs={{0,16},{1,17},{2,18},{3,19},{4,20},{5,21},{6,22},{7,23},{8,24},{9,... | collective-permute-start | bytes 5677064 | tf_op jit(solution)/shard_map/ppermute | solution.py:731
  273.4 1.5 copy-start
Sparse Core Ops, SparseCore 0:
  122.6 103.9 all-gather.2

commit v2 on v1

--- a/solution.py
+++ b/solution.py
@@ -463,7 +463,7 @@
 
     @pl.when(coarse)
     def _():
-        @pl.loop(0, plan.pairs, unroll=2)
+        @pl.loop(0, plan.pairs, unroll=8)
         def _(xp):
             emit(xp, dot(wide[...], spread(xp, 4 * modes)))
 
@@ -471,7 +471,7 @@
     def _():
         c2 = lax.rem(step, 2)
 
-        @pl.loop(0, plan.pairs, unroll=2)
+        @pl.loop(0, plan.pairs, unroll=8)
         def _(xp):
             at = pl.multiple_of((c2 * plan.pairs + xp) * half, 16)
             table = interp[c2 * plan.pairs + xp]

time: 354 us -> 349 us (0.986)
  Pallas kernels: 178 us -> 167 us
  waiting for transfers between devices: 75.2 us -> 81.5 us
    pallas_call x13, Pallas kernels: 178 us -> 167 us  [call(): pl.pallas_call(run, grid=grid, in_specs=in_specs + [pl.BlockSpec(memory_s...]
    ppermute x2, waiting for transfers between devices: 0.01 us -> 6.26 us  [fast_body(): seconds.append(lax.ppermute(last, 'pool', [(0, 1)]))]
  transfers between devices with their start and end apart: 17 -> 17, of which waited for: 4 -> 5; matrix products, arithmetic and copies ran while one was open for 4% -> 4% of each run, Pallas kernels for 42% -> 41%
where the time goes in v2:
time: 349 us; the launch traced here: 348 us
  Pallas kernels  167 us (48%)
  waiting for transfers between devices  81.5 us (23%)
  starting transfers between devices  68 us (19%)
  local copies, waits for them, and re-layouts  16 us (5%)
  between operations  13.6 us (4%)
    pallas_call x13, Pallas kernels, call(): pl.pallas_call(run, grid=grid, in_specs=in_specs + [pl.BlockSpec(memory_s...  167 us
    all_gather x1, waiting for transfers between devices, fast_body(): here = lax.all_gather(here, 'slab', axis=0, tiled=False)  36.3 us
    ppermute x1, starting transfers between devices, fast_body(): gathered = [here, lax.ppermute(over, 'pool', [(1, 0)])]  35.1 us
    ppermute x2, waiting for transfers between devices, fast_body(): firsts.append(lax.ppermute(last, 'pool', [(0, 1)]))  24.8 us
    all_to_all x1, waiting for transfers between devices, fast_body(): lax.all_to_all(sent, 'slab', split_axis=0, concat_axis=0, tiled=True)  14 us
    all_to_all x1, starting transfers between devices, fast_body(): lax.all_to_all(back, 'slab', split_axis=0, concat_axis=0, tiled=True)  7.37 us
  transfers between devices with their start and end apart: 17, of which 5 were waited for; matrix products, arithmetic and copies ran while one was open for 4% of the time, Pallas kernels for 41%

profile of v2, /device:TPU:18, one launch (start us, length us, event | category | flops | bytes accessed | tf_op | source)
XLA Modules:
  0.0 347.5 jit_solution(673446097989170444)
XLA Ops:
  6.5 3.4 collective-permute-start.1
  10.0 2.5 collective-permute-start
  12.5 13.6 %shard_map.172.refs_0_ = bf16[8,10,32,512]{3,2,1,0:T(8,128)(2,1)} custom-call(bf16[64,224]{1,0:T(8,128)(2,1)} %constant.57.clone.refs_0_, bf16[256,128]{1,0:T(8,128)(2,1)} %constant.58.clone.refs_1_, bf16[10,32,224,128]{3,2,1,0:T(8,128)(2,1)} %bitcast.26), custom_call_target="tpu_custom_call" | custom-call | flops 1000 | bytes 1000 | tf_op jit(solution)/shard_map/pallas_call | solution.py:518
  26.7 6.0 %all-to-all-start = ((bf16[8,10,32,512]{3,2,1,0:T(8,128)(2,1)}), bf16[8,10,32,512]{3,2,1,0:T(8,128)(2,1)}, u32[]{:S(2)}, u32[]{:S(2)}) async-start(bf16[8,10,32,512]{3,2,1,0:T(8,128)(2,1)} %shard_map.173.refs_3_), calls=%async_computation | async-start | bytes 5242880 | tf_op jit(solution)/shard_map/all_to_all | solution.py:696
  32.8 10.1 %shard_map.174.refs_3_ = bf16[3,3696,128]{2,1,0:T(8,128)(2,1)} custom-call(s32[26]{0:T(128)} %concatenate.3.refs_1_.refs_0_, bf16[32,256,128]{2,1,0:T(8,128)(2,1)} %constant.59.clone.refs_1_, bf16[10,32,224,128]{3,2,1,0:T(8,128)(2,1)} %bitcast.27, bf16[8,10,32,512]{3,2,1,0:T(8,128)(2,1)} %shard_map.173.refs_3_), custom_call_target="tpu_custom_call" | custom-call | flops 1000 | bytes 1000 | tf_op jit(solution)/shard_map/pallas_call | solution.py:518
  44.1 11.2 %shard_map.175 = (bf16[3,3696,128]{2,1,0:T(8,128)(2,1)}, bf16[3,1856,128]{2,1,0:T(8,128)(2,1)}, bf16[3,1856,128]{2,1,0:T(8,128)(2,1)}) custom-call(s32[26]{0:T(128)} %concatenate.3.refs_1_.refs_0_, bf16[32,256,128]{2,1,0:T(8,128)(2,1)} %constant.59.clone.refs_1_, bf16[10,32,224,128]{3,2,1,0:T(8,128)(2,1)} %bitcast.28, bf16[3,3696,128]{2,1,0:T(8,128)(2,1)} %shard_map.174.refs_3_), custom_call_target="tpu_custom_call" | custom-call | flops 1000 | bytes 1000 | tf_op jit(solution)/shard_map/pallas_call | solution.py:518
  55.3 1.8 collective-permute-start.8
  57.0 7.8 %shard_map.176.refs_3_ = bf16[2,3696,128]{2,1,0:T(8,128)(2,1)} custom-call(s32[26]{0:T(128)} %concatenate.3.refs_1_.refs_0_, bf16[32,256,128]{2,1,0:T(8,128)(2,1)} %constant.59.clone.refs_1_, bf16[10,32,224,128]{3,2,1,0:T(8,128)(2,1)} %bitcast.29, bf16[3,3696,128]{2,1,0:T(8,128)(2,1)} %get-tuple-element.11.refs_3_.refs_1_), custom_call_target="tpu_custom_call" | custom-call | flops 1000 | bytes 1000 | tf_op jit(solution)/shard_map/pallas_call | solution.py:518
  64.8 1.8 collective-permute-start.9
  66.6 8.5 %shard_map.177 = (bf16[2,3696,128]{2,1,0:T(8,128)(2,1)}, bf16[2,1856,128]{2,1,0:T(8,128)(2,1)}, bf16[2,1856,128]{2,1,0:T(8,128)(2,1)}) custom-call(s32[26]{0:T(128)} %concatenate.3.refs_1_.refs_0_, bf16[32,256,128]{2,1,0:T(8,128)(2,1)} %constant.59.clone.refs_1_, bf16[10,32,224,128]{3,2,1,0:T(8,128)(2,1)} %bitcast.30, bf16[2,3696,128]{2,1,0:T(8,128)(2,1)} %shard_map.176.refs_3_), custom_call_target="tpu_custom_call" | custom-call | flops 1000 | bytes 1000 | tf_op jit(solution)/shard_map/pallas_call | solution.py:518
  75.1 14.0 %all-to-all-done.refs_2_ = bf16[8,10,32,512]{3,2,1,0:T(8,128)(2,1)} async-done(((bf16[8,10,32,512]{3,2,1,0:T(8,128)(2,1)}), bf16[8,10,32,512]{3,2,1,0:T(8,128)(2,1)}, u32[]{:S(2)}, u32[]{:S(2)}) %all-to-all-start) | async-done | bytes 2621472 | tf_op jit(solution)/shard_map/all_to_all | solution.py:696
  89.1 10.2 %shard_map.178 = bf16[20,64,512]{2,1,0:T(8,128)(2,1)} custom-call(bf16[64,256]{1,0:T(8,128)(2,1)} %constant.60.clone.refs_0_, bf16[10,20,64,512]{3,2,1,0:T(8,128)(2,1)} %bitcast.32, bf16[8,10,32,512]{3,2,1,0:T(8,128)(2,1)} %all-to-all-done.refs_2_, bf16[2,3696,128]{2,1,0:T(8,128)(2,1)} %get-tuple-element.12.refs_3_.refs_1_), custom_call_target="tpu_custom_call" | custom-call | flops 1000 | bytes 1000 | tf_op jit(solution)/shard_map/pallas_call | solution.py:518
  99.2 2.2 dynamic-slice_bitcast_fusion
  101.5 6.3 %collective-permute-done.4.refs_2_.refs_7_ = bf16[3,3696,128]{2,1,0:T(8,128)(2,1)S(1)} collective-permute-done((bf16[3,3696,128]{2,1,0:T(8,128)(2,1)}, bf16[3,3696,128]{2,1,0:T(8,128)(2,1)S(1)}, u32[]{:S(2)}, u32[]{:S(2)}) %collective-permute-start.4) | collective-permute-done | bytes 2838560 | tf_op jit(solution)/shard_map/ppermute | solution.py:702
  107.7 1.6 copy-done.1
  109.5 2.3 shard_map.179.refs_1_
  112.9 1.6 collective-permute-start.11
  114.5 7.2 %shard_map.180.refs_5_.refs_1_ = bf16[8,10,32,512]{3,2,1,0:T(8,128)(2,1)} custom-call(bf16[256,64]{1,0:T(8,128)(2,1)} %constant.61.clone.refs_0_, bf16[10,64,512]{2,1,0:T(8,128)(2,1)} %shard_map.179.refs_1_), custom_call_target="tpu_custom_call" | custom-call | flops 1000 | bytes 1000 | tf_op jit(solution)/shard_map/pallas_call | solution.py:518
  123.8 7.4 %all-to-all-start.1 = ((bf16[8,10,32,512]{3,2,1,0:T(8,128)(2,1)}), bf16[8,10,32,512]{3,2,1,0:T(8,128)(2,1)S(1)}, u32[]{:S(2)}, u32[]{:S(2)}) async-start(bf16[8,10,32,512]{3,2,1,0:T(8,128)(2,1)} %shard_map.180.refs_5_.refs_1_), calls=%async_computation.1 | async-start | bytes 5242880 | tf_op jit(solution)/shard_map/all_to_all | solution.py:717
  132.5 2.3 reshape.22
  135.3 1.6 collective-permute-start.6
  136.9 1.7 collective-permute-start.7
  140.0 22.8 %shard_map.181.refs_4_.refs_6_ = bf16[10,32,224,128]{3,2,1,0:T(8,128)(2,1)} custom-call(bf16[160,160]{1,0:T(8,128)(2,1)} %get-tuple-element.22.refs_0_, bf16[160,160]{1,0:T(8,128)(2,1)} %get-tuple-element.21.refs_1_, f32[160,256]{1,0:T(8,128)} %broadcast_in_dim.21.refs_2_, bf16[10,32,224,128]{3,2,1,0:T(8,128)(2,1)} %bitcast.31, ...), custom_call_target="tpu_custom_call" | custom-call | flops 1000 | bytes 1000 | tf_op jit(solution)/shard_map/pallas_call | solution.py:518
  162.8 18.6 %collective-permute-done.5.refs_5_.refs_7_ = bf16[2,3696,128]{2,1,0:T(8,128)(2,1)} collective-permute-done((bf16[2,3696,128]{2,1,0:T(8,128)(2,1)}, bf16[2,3696,128]{2,1,0:T(8,128)(2,1)}, u32[]{:S(2)}, u32[]{:S(2)}) %collective-permute-start.5) | collective-permute-done | bytes 1892384 | tf_op jit(solution)/shard_map/ppermute | solution.py:702
  181.3 7.6 %shard_map.182.refs_4_ = bf16[3,3696,128]{2,1,0:T(8,128)(2,1)} custom-call(s32[26]{0:T(128)} %concatenate.3.refs_1_.refs_0_, bf16[3,3696,128]{2,1,0:T(8,128)(2,1)} %get-tuple-element.11.refs_3_.refs_1_, bf16[3,1856,128]{2,1,0:T(8,128)(2,1)} %collective-permute-done.8.refs_2_, bf16[3,1856,128]{2,1,0:T(8,128)(2,1)} %collective-permute-done.9.refs_3_, ...), custom_call_target="tpu_custom_call" | custom-call | flops 1000 | bytes 1000 | tf_op jit(solution)/shard_map/pallas_call | solution.py:518
  190.2 36.3 %all-gather.3.cloned.1.call-done = bf16[48,64,512]{2,1,0:T(8,128)(2,1)} async-done(((bf16[6,64,512]{2,1,0:T(8,128)(2,1)}), bf16[48,64,512]{2,1,0:T(8,128)(2,1)}) %all-gather.3.cloned.1.call-update) | async-done | bytes 3145744 | tf_op jit(solution)/shard_map/all_gather | solution.py:727
  226.6 3.1 slice.14.refs_0_
  229.7 5.9 %shard_map.183.refs_1_ = bf16[2,3696,128]{2,1,0:T(8,128)(2,1)} custom-call(s32[26]{0:T(128)} %concatenate.3.refs_1_.refs_0_, bf16[2,3696,128]{2,1,0:T(8,128)(2,1)} %get-tuple-element.12.refs_3_.refs_1_, bf16[2,1856,128]{2,1,0:T(8,128)(2,1)} %collective-permute-done.6.refs_2_, bf16[2,1856,128]{2,1,0:T(8,128)(2,1)} %collective-permute-done.7.refs_3_, ...), custom_call_target="tpu_custom_call" | custom-call | flops 1000 | bytes 1000 | tf_op jit(solution)/shard_map/pallas_call | solution.py:518
  235.6 35.1 %collective-permute-start.12 = (bf16[8,4,64,512]{3,2,1,0:T(8,128)(2,1)}, bf16[8,4,64,512]{3,2,1,0:T(8,128)(2,1)}, u32[]{:S(2)}, u32[]{:S(2)}) collective-permute-start(bf16[8,4,64,512]{3,2,1,0:T(8,128)(2,1)} %shard_map.185), channel_id=1, source_target_pairs={{16,0},{17,1},{18,2},{19,3},{20,4},{21,5},{22,6},{23,7},{24,8},{25... | collective-permute-start | bytes 6291464 | tf_op jit(solution)/shard_map/ppermute | solution.py:733
  274.9 34.7 %shard_map.186.refs_11_ = bf16[10,32,224,128]{3,2,1,0:T(8,128)(2,1)} custom-call(s32[26]{0:T(128)} %concatenate.3.refs_1_.refs_0_, bf16[128,256]{1,0:T(8,128)(2,1)} %constant.63.clone.refs_1_, bf16[128,256]{1,0:T(8,128)(2,1)} %constant.64.clone.refs_2_, bf16[96,64]{1,0:T(8,128)(2,1)} %bitcast.36, bf16[224,64]{1,0:T(8,128)(2,1)} %constant.65.clone.refs_4_, ...), custom_call_target="tpu_custom_call" | custom-call | flops 1000 | bytes 1000 | tf_op jit(solution)/shard_map/pallas_call | solution.py:518
  309.6 6.3 %collective-permute-done.10.refs_8_ = bf16[2,3696,128]{2,1,0:T(8,128)(2,1)} collective-permute-done((bf16[2,3696,128]{2,1,0:T(8,128)(2,1)}, bf16[2,3696,128]{2,1,0:T(8,128)(2,1)}, u32[]{:S(2)}, u32[]{:S(2)}) %collective-permute-start.10) | collective-permute-done | bytes 1892384 | tf_op jit(solution)/shard_map/ppermute | solution.py:731
  315.8 24.8 %shard_map.187 = bf16[10,32,224,128]{3,2,1,0:T(8,128)(2,1)} custom-call(s32[26]{0:T(128)} %concatenate.3.refs_1_.refs_0_, bf16[128,256]{1,0:T(8,128)(2,1)} %constant.63.clone.refs_1_, bf16[128,256]{1,0:T(8,128)(2,1)} %constant.64.clone.refs_2_, bf16[96,64]{1,0:T(8,128)(2,1)} %bitcast.37, ...), custom_call_target="tpu_custom_call", output_to_operand_aliasing={{}: (11, {})} | custom-call | flops 1000 | bytes 1000 | tf_op jit(solution)/shard_map/pallas_call | solution.py:518
  (51 shorter events, 13.9 us)
Async XLA Ops:
  6.5 132.7 %collective-permute-start.2 = (bf16[10,32,224,128]{3,2,1,0:T(8,128)(2,1)}, bf16[10,32,224,128]{3,2,1,0:T(8,128)(2,1)}, u32[]{:S(2)}, u32[]{:S(2)}) collective-permute-start(bf16[10,32,224,128]{3,2,1,0:T(8,128)(2,1)} %bitcast.25), channel_id=1, source_target_pairs={{0,1},{1,0},{2,3},{3,2},{4,5},{5,4},{6,7},{7,6},{8,9},{9,8},{10,11... | collective-permute-start | bytes 55050248 | tf_op jit(solution)/shard_map/ppermute | solution.py:31
  6.5 19.6 %copy-start.5 = (s32[1,8]{1,0:T(1,128)S(1)}, s32[1,8]{1,0:T(1,128)}, u32[]{:S(2)}) copy-start(s32[1,8]{1,0:T(1,128)} %param.22) | copy-start | bytes 100
  6.5 19.5 %collective-permute-start.1 = (s32[8]{0:T(128)}, s32[8]{0:T(128)S(1)}, u32[]{:S(2)}, u32[]{:S(2)}) collective-permute-start(s32[8]{0:T(128)} %bitcast.38), channel_id=1, source_target_pairs={{2,0},{4,2},{6,4},{8,6},{10,8},{12,10},{14,12},{3,1},{5,3},{7,5},{... | collective-permute-start | bytes 104 | tf_op jit(solution)/shard_map/ppermute | solution.py:25
  10.0 16.1 %collective-permute-start = (s32[8]{0:T(128)}, s32[8]{0:T(128)S(1)}, u32[]{:S(2)}, u32[]{:S(2)}) collective-permute-start(s32[8]{0:T(128)} %bitcast.39), channel_id=1, source_target_pairs={{0,2},{2,4},{4,6},{6,8},{8,10},{10,12},{12,14},{1,3},{3,5},{5,7},{... | collective-permute-start | bytes 104 | tf_op jit(solution)/shard_map/ppermute | solution.py:25
  26.7 62.4 %all-to-all-start = ((bf16[8,10,32,512]{3,2,1,0:T(8,128)(2,1)}), bf16[8,10,32,512]{3,2,1,0:T(8,128)(2,1)}, u32[]{:S(2)}, u32[]{:S(2)}) async-start(bf16[8,10,32,512]{3,2,1,0:T(8,128)(2,1)} %shard_map.173.refs_3_), calls=%async_computation | async-start | bytes 5242880 | tf_op jit(solution)/shard_map/all_to_all | solution.py:696
  32.8 193.8 %all-gather.3.cloned.1.call-start = ((), (), s32[]{:S(2)}) async-start(), calls=%async_computation.2 | async-start | bytes 3538944 | tf_op jit(solution)/shard_map/all_gather | solution.py:727
  42.8 64.9 %collective-permute-start.4 = (bf16[3,3696,128]{2,1,0:T(8,128)(2,1)}, bf16[3,3696,128]{2,1,0:T(8,128)(2,1)S(1)}, u32[]{:S(2)}, u32[]{:S(2)}) collective-permute-start(bf16[3,3696,128]{2,1,0:T(8,128)(2,1)} %shard_map.174.refs_3_), channel_id=1, source_target_pairs={{0,16},{1,17},{2,18},{3,19},{4,20},{5,21},{6,22},{7,23},{8,24},{9,... | collective-permute-start | bytes 8515592 | tf_op jit(solution)/shard_map/ppermute | solution.py:702
  55.3 67.2 %collective-permute-start.8 = (bf16[3,1856,128]{2,1,0:T(8,128)(2,1)}, bf16[3,1856,128]{2,1,0:T(8,128)(2,1)}, u32[]{:S(2)}, u32[]{:S(2)}) collective-permute-start(bf16[3,1856,128]{2,1,0:T(8,128)(2,1)} %get-tuple-element.15), channel_id=1, source_target_pairs={{0,2},{2,4},{4,6},{6,8},{8,10},{10,12},{12,14},{1,3},{3,5},{5,7},{... | collective-permute-start | bytes 4276232 | tf_op jit(solution)/shard_map/ppermute | solution.py:706
  64.8 57.7 %collective-permute-start.9 = (bf16[3,1856,128]{2,1,0:T(8,128)(2,1)}, bf16[3,1856,128]{2,1,0:T(8,128)(2,1)}, u32[]{:S(2)}, u32[]{:S(2)}) collective-permute-start(bf16[3,1856,128]{2,1,0:T(8,128)(2,1)} %get-tuple-element.16), channel_id=1, source_target_pairs={{2,0},{4,2},{6,4},{8,6},{10,8},{12,10},{14,12},{3,1},{5,3},{7,5},{... | collective-permute-start | bytes 4276232 | tf_op jit(solution)/shard_map/ppermute | solution.py:707
  101.5 6.3 %collective-permute-start.3 = (bf16[10,64,512]{2,1,0:T(8,128)(2,1)S(1)}, bf16[10,64,512]{2,1,0:T(8,128)(2,1)S(1)}, u32[]{:S(2)}, u32[]{:S(2)}) collective-permute-start(bf16[10,64,512]{2,1,0:T(8,128)(2,1)S(1)} %get-tuple-element.17), channel_id=1, source_target_pairs={{0,1},{1,0},{2,3},{3,2},{4,5},{5,4},{6,7},{7,6},{8,9},{9,8},{10,11... | collective-permute-start | bytes 1966088 | tf_op jit(solution)/shard_map/ppermute | solution.py:31
  107.7 1.6 copy-start.1
  107.7 1.8 copy-start.3
  111.8 9.9 %copy-start.2 = (bf16[10,64,512]{2,1,0:T(8,128)(2,1)S(1)}, bf16[10,64,512]{2,1,0:T(8,128)(2,1)}, u32[]{:S(2)}) copy-start(bf16[10,64,512]{2,1,0:T(8,128)(2,1)} %shard_map.179.refs_1_) | copy-start | bytes 1966084
  112.9 8.8 %collective-permute-start.11 = (bf16[6,64,512]{2,1,0:T(8,128)(2,1)S(1)}, bf16[6,64,512]{2,1,0:T(8,128)(2,1)S(1)}, u32[]{:S(2)}, u32[]{:S(2)}) collective-permute-start(bf16[6,64,512]{2,1,0:T(8,128)(2,1)S(1)} %slice.12), channel_id=1, source_target_pairs={{16,0},{17,1},{18,2},{19,3},{20,4},{21,5},{22,6},{23,7},{24,8},{25... | collective-permute-start | bytes 1179656 | tf_op jit(solution)/shard_map/ppermute | solution.py:724
  122.5 8.7 %copy-start.6 = (bf16[1,10]{1,0:T(2,128)(2,1)S(1)}, bf16[1,10]{1,0:T(2,128)(2,1)}, u32[]{:S(2)}) copy-start(bf16[1,10]{1,0:T(2,128)(2,1)} %param.21) | copy-start | bytes 64
  122.5 8.9 %copy-start.4 = (bf16[1,20,10]{1,2,0:T(8,128)(2,1)S(1)}, bf16[1,20,10]{1,2,0:T(8,128)(2,1)}, u32[]{:S(2)}) copy-start(bf16[1,20,10]{1,2,0:T(8,128)(2,1)} %param.20) | copy-start | bytes 1204
  122.5 58.8 %collective-permute-start.5 = (bf16[2,3696,128]{2,1,0:T(8,128)(2,1)}, bf16[2,3696,128]{2,1,0:T(8,128)(2,1)}, u32[]{:S(2)}, u32[]{:S(2)}) collective-permute-start(bf16[2,3696,128]{2,1,0:T(8,128)(2,1)} %shard_map.176.refs_3_), channel_id=1, source_target_pairs={{0,16},{1,17},{2,18},{3,19},{4,20},{5,21},{6,22},{7,23},{8,24},{9,... | collective-permute-start | bytes 5677064 | tf_op jit(solution)/shard_map/ppermute | solution.py:702
  123.8 149.6 %all-to-all-start.1 = ((bf16[8,10,32,512]{3,2,1,0:T(8,128)(2,1)}), bf16[8,10,32,512]{3,2,1,0:T(8,128)(2,1)S(1)}, u32[]{:S(2)}, u32[]{:S(2)}) async-start(bf16[8,10,32,512]{3,2,1,0:T(8,128)(2,1)} %shard_map.180.refs_5_.refs_1_), calls=%async_computation.1 | async-start | bytes 5242880 | tf_op jit(solution)/shard_map/all_to_all | solution.py:717
  135.3 94.4 %collective-permute-start.6 = (bf16[2,1856,128]{2,1,0:T(8,128)(2,1)}, bf16[2,1856,128]{2,1,0:T(8,128)(2,1)}, u32[]{:S(2)}, u32[]{:S(2)}) collective-permute-start(bf16[2,1856,128]{2,1,0:T(8,128)(2,1)} %get-tuple-element.13), channel_id=1, source_target_pairs={{0,2},{2,4},{4,6},{6,8},{8,10},{10,12},{12,14},{1,3},{3,5},{5,7},{... | collective-permute-start | bytes 2850824 | tf_op jit(solution)/shard_map/ppermute | solution.py:706
  136.9 92.8 %collective-permute-start.7 = (bf16[2,1856,128]{2,1,0:T(8,128)(2,1)}, bf16[2,1856,128]{2,1,0:T(8,128)(2,1)}, u32[]{:S(2)}, u32[]{:S(2)}) collective-permute-start(bf16[2,1856,128]{2,1,0:T(8,128)(2,1)} %get-tuple-element.14), channel_id=1, source_target_pairs={{2,0},{4,2},{6,4},{8,6},{10,8},{12,10},{14,12},{3,1},{5,3},{7,5},{... | collective-permute-start | bytes 2850824 | tf_op jit(solution)/shard_map/ppermute | solution.py:707
  188.9 84.4 %collective-permute-start.13 = (bf16[3,3696,128]{2,1,0:T(8,128)(2,1)}, bf16[3,3696,128]{2,1,0:T(8,128)(2,1)}, u32[]{:S(2)}, u32[]{:S(2)}) collective-permute-start(bf16[3,3696,128]{2,1,0:T(8,128)(2,1)} %shard_map.182.refs_4_), channel_id=1, source_target_pairs={{0,16},{1,17},{2,18},{3,19},{4,20},{5,21},{6,22},{7,23},{8,24},{9,... | collective-permute-start | bytes 8515592 | tf_op jit(solution)/shard_map/ppermute | solution.py:731
  235.6 80.2 %collective-permute-start.12 = (bf16[8,4,64,512]{3,2,1,0:T(8,128)(2,1)}, bf16[8,4,64,512]{3,2,1,0:T(8,128)(2,1)}, u32[]{:S(2)}, u32[]{:S(2)}) collective-permute-start(bf16[8,4,64,512]{3,2,1,0:T(8,128)(2,1)} %shard_map.185), channel_id=1, source_target_pairs={{16,0},{17,1},{18,2},{19,3},{20,4},{21,5},{22,6},{23,7},{24,8},{25... | collective-permute-start | bytes 6291464 | tf_op jit(solution)/shard_map/ppermute | solution.py:733
  270.7 45.1 %collective-permute-start.10 = (bf16[2,3696,128]{2,1,0:T(8,128)(2,1)}, bf16[2,3696,128]{2,1,0:T(8,128)(2,1)}, u32[]{:S(2)}, u32[]{:S(2)}) collective-permute-start(bf16[2,3696,128]{2,1,0:T(8,128)(2,1)} %shard_map.183.refs_1_), channel_id=1, source_target_pairs={{0,16},{1,17},{2,18},{3,19},{4,20},{5,21},{6,22},{7,23},{8,24},{9,... | collective-permute-start | bytes 5677064 | tf_op jit(solution)/shard_map/ppermute | solution.py:731
  273.4 1.5 copy-start
Sparse Core Ops, SparseCore 0:
  122.6 103.9 all-gather.2

commit v3 on v2

--- a/solution.py
+++ b/solution.py
@@ -239,54 +239,40 @@
     return chosen(same & near & (by_block(block, info["place"]) == slot)).astype(BF)
 
 
-def pack_first_kernel(plan, meta, esel, u, h1, sel):
-    half = plan.half
+def pack_kernel(plan, meta, esel, u, h1, h2, right, left, sel):
+    half, hop, nb = plan.half, plan.hop, plan.blocks
+    pad = plan.edge_rows
 
     @pl.when(pl.program_id(0) == 0)
     def _():
-        sel[...] = picks(plan, listing(meta, plan), 0)
-
-    def store(c2, double, tiles):
-        for i, tile in enumerate(tiles):
-            at = (c2 * plan.pairs + 2 * double + i) * half
-            h1[0, at:at + half, :] = tile.astype(BF)
-
-    def store_edges(packed):
-        h1[0, plan.mid_rows:] = packed
-
-    pack(plan, sel, esel, u, store, store_edges)
-
-
-def pack_rest_kernel(plan, meta, esel, u, h2, right, left, sel):
-    half, hop, nb = plan.half, plan.hop, plan.blocks
-    pad = plan.edge_rows
-
-    @pl.when(pl.program_id(0) == 0)
-    def _():
-        sel[0:half] = picks(plan, listing(meta, plan), nb - 2 * HOP)
+        info = listing(meta, plan)
+        sel[0:half] = picks(plan, info, 0)
+        sel[half:2 * half] = picks(plan, info, nb - 2 * HOP)
         row, col = row_col(pad, plan.ny)
         block = steps_of(col, plan.rows, nb)
         slot = steps_of(row, plan.rows, HOP + 1)
         same = (row - slot * plan.rows == col - block * plan.rows) & (slot < HOP)
         for which in range(2):
             rank = by_block(block, sends(meta, plan, 2 - which))
-            start = half + which * pad
+            start = 2 * half + which * pad
             sel[start:start + pad] = chosen(same & (rank == slot)).astype(BF)
 
     def store(c2, double, tiles):
         for i, tile in enumerate(tiles):
             at = (c2 * plan.pairs + 2 * double + i) * half
-            h2[0, at:at + half, :] = tile[0:half].astype(BF)
+            h1[0, at:at + half, :] = tile[0:half].astype(BF)
+            h2[0, at:at + half, :] = tile[half:2 * half].astype(BF)
         at = (c2 * plan.pairs // 2 + double) * 2 * hop
-        for ref, start in ((right, half), (left, half + pad)):
+        for ref, start in ((right, 2 * half), (left, 2 * half + pad)):
             ref[0, at:at + 2 * hop, :] = jnp.concatenate(
                 [tile[start:start + hop] for tile in tiles], axis=0
             ).astype(BF)
 
     def store_edges(packed):
-        h2[0, plan.mid_rows:] = packed[0:half]
-        right[0, 2 * plan.pairs * hop:] = packed[half:half + pad]
-        left[0, 2 * plan.pairs * hop:] = packed[half + pad:half + 2 * pad]
+        h1[0, plan.mid_rows:] = packed[0:half]
+        h2[0, plan.mid_rows:] = packed[half:2 * half]
+        right[0, 2 * plan.pairs * hop:] = packed[2 * half:2 * half + pad]
+        left[0, 2 * plan.pairs * hop:] = packed[2 * half + pad:2 * half + 2 * pad]
 
     pack(plan, sel, esel, u, store, store_edges)
 
@@ -323,7 +309,7 @@
             sel[offset] = build(2 * hop, hop, offset)
         edge_sel[...] = build(pad, pad, 0)
 
-    @pl.loop(0, plan.pairs, unroll=4)
+    @pl.loop(0, plan.pairs, unroll=16)
     def _(double):
         at = pl.multiple_of(double * 2 * hop, 16)
         sides = jnp.concatenate(
@@ -553,18 +539,17 @@
     )
 
 
-def run_pack(plan, meta, esel, field, group, near, after=()):
+def run_pack(plan, meta, esel, field, group, after=()):
     start, count = group
     full = jax.ShapeDtypeStruct((count, plan.pack_rows, LANES), BF)
     part = jax.ShapeDtypeStruct((count, plan.nb_rows, LANES), BF)
-    shapes = [full, part, part] if near else [full]
-    rows = plan.half + 2 * plan.edge_rows if near else plan.half
+    shapes = [full, full, part, part]
     return call(
-        pack_rest_kernel if near else pack_first_kernel, plan, (count,),
+        pack_kernel, plan, (count,),
         [SCALARS, whole(esel.shape),
          pl.BlockSpec((2,) + field.shape[1:], lambda c: (c + start, 0, 0, 0))],
         [pl.BlockSpec((1,) + shape.shape[1:], lambda c: (c, 0, 0)) for shape in shapes], shapes,
-        [pltpu.VMEM((rows, plan.ny), BF)],
+        [pltpu.VMEM((2 * plan.half + 2 * plan.edge_rows, plan.ny), BF)],
         (10**9, field.size * 3, 0), (meta, esel, field), after,
     )
 
@@ -698,9 +683,8 @@
     both = ("pool", "slab")
     firsts, packs, last = [], [], sent
     for group in plan.groups:
-        last = run_pack(plan, meta, esel, field, group, False, (last,))[0]
-        firsts.append(lax.ppermute(last, "pool", [(0, 1)]))
-        last, to_right, to_left = run_pack(plan, meta, esel, field, group, True, (last,))
+        lead, last, to_right, to_left = run_pack(plan, meta, esel, field, group, (last,))
+        firsts.append(lax.ppermute(lead, "pool", [(0, 1)]))
         packs.append((
             last,
             lax.ppermute(to_right, both, [(i, i + 1) for i in range(slabs - 1)]),
@@ -729,8 +713,7 @@
     for second, from_left, from_right in packs:
         last = run_assemble(plan, meta, second, from_left, from_right, (last, firsts[-1]))
         seconds.append(lax.ppermute(last, "pool", [(0, 1)]))
-    over = gate(here[:, lead - rest:], (last,))
-    gathered = [here, lax.ppermute(over, "pool", [(1, 0)])]
+    gathered = [here, lax.ppermute(here[:, lead - rest:], "pool", [(1, 0)])]
 
     to_coarse = 0.5 * host_interp(plan.nz)
     gzp = (inv_z.T.astype(np.float32) @ to_coarse).astype(ml_dtypes.bfloat16)

time: 349 us -> 336 us (0.963)
  waiting for transfers between devices: 81.5 us -> 104 us
  Pallas kernels: 167 us -> 148 us
  starting transfers between devices: 68 us -> 50.7 us
    pallas_call x13 -> x11, Pallas kernels: 167 us -> 148 us  [call(): pl.pallas_call(run, grid=grid, in_specs=in_specs + [pl.BlockSpec(memory_s...]
    all_to_all x1, waiting for transfers between devices: 14 us -> 30.1 us  [fast_body(): lax.all_to_all(sent, 'slab', split_axis=0, concat_axis=0, tiled=True)]
    ppermute x3, starting transfers between devices: 37.7 us -> 21.8 us  [the longest x1 19.2 us: fast_body(): gathered = [here, lax.ppermute(here[:, lead - rest:], 'pool', [(1, 0)])]]
    all_gather x1, waiting for transfers between devices: 36.3 us -> 44.4 us  [fast_body(): here = lax.all_gather(here, 'slab', axis=0, tiled=False)]
    ppermute x3, waiting for transfers between devices: 24.8 us -> 18.7 us  [the longest x2 18.2 us: fast_body(): firsts.append(lax.ppermute(lead, 'pool', [(0, 1)]))]
    ppermute x2, waiting for transfers between devices: 6.26 us -> 10.9 us  [fast_body(): seconds.append(lax.ppermute(last, 'pool', [(0, 1)]))]
  transfers between devices with their start and end apart: 17 -> 17, of which waited for: 5 -> 6; matrix products, arithmetic and copies ran while one was open for 4% -> 4% of each run, Pallas kernels for 41% -> 37%
where the time goes in v3:
time: 336 us; the launch traced here: 334 us
  Pallas kernels  148 us (44%)
  waiting for transfers between devices  104 us (31%)
  starting transfers between devices  50.7 us (15%)
  local copies, waits for them, and re-layouts  16 us (5%)
  between operations  13.6 us (4%)
    pallas_call x11, Pallas kernels, call(): pl.pallas_call(run, grid=grid, in_specs=in_specs + [pl.BlockSpec(memory_s...  148 us
    all_gather x1, waiting for transfers between devices, fast_body(): here = lax.all_gather(here, 'slab', axis=0, tiled=False)  44.4 us
    all_to_all x1, waiting for transfers between devices, fast_body(): lax.all_to_all(sent, 'slab', split_axis=0, concat_axis=0, tiled=True)  30.1 us
    ppermute x1, starting transfers between devices, fast_body(): gathered = [here, lax.ppermute(here[:, lead - rest:], 'pool', [(1, 0)])]  19.2 us
    ppermute x2, waiting for transfers between devices, fast_body(): firsts.append(lax.ppermute(lead, 'pool', [(0, 1)]))  18.2 us
    ppermute x2, waiting for transfers between devices, fast_body(): seconds.append(lax.ppermute(last, 'pool', [(0, 1)]))  10.9 us
  transfers between devices with their start and end apart: 17, of which 6 were waited for; matrix products, arithmetic and copies ran while one was open for 4% of the time, Pallas kernels for 37%

profile of v3, /device:TPU:18, one launch (start us, length us, event | category | flops | bytes accessed | tf_op | source)
XLA Modules:
  0.0 334.4 jit_solution(8336425093301793070)
XLA Ops:
  6.5 3.4 %collective-permute-start.1 = (s32[8]{0:T(128)}, s32[8]{0:T(128)S(1)}, u32[]{:S(2)}, u32[]{:S(2)}) collective-permute-start(s32[8]{0:T(128)} %bitcast.36), channel_id=1, source_target_pairs={{2,0},{4,2},{6,4},{8,6},{10,8},{12,10},{14,12},{3,1},{5,3},{7,5},{... | collective-permute-start | bytes 104 | tf_op jit(solution)/shard_map/ppermute | solution.py:25
  10.0 2.5 collective-permute-start
  12.5 13.6 %shard_map.172.refs_0_ = bf16[8,10,32,512]{3,2,1,0:T(8,128)(2,1)} custom-call(bf16[64,224]{1,0:T(8,128)(2,1)} %constant.57.clone.refs_0_, bf16[256,128]{1,0:T(8,128)(2,1)} %constant.58.clone.refs_1_, bf16[10,32,224,128]{3,2,1,0:T(8,128)(2,1)} %bitcast.26), custom_call_target="tpu_custom_call" | custom-call | flops 1000 | bytes 1000 | tf_op jit(solution)/shard_map/pallas_call | solution.py:504
  26.7 6.0 %all-to-all-start = ((bf16[8,10,32,512]{3,2,1,0:T(8,128)(2,1)}), bf16[8,10,32,512]{3,2,1,0:T(8,128)(2,1)}, u32[]{:S(2)}, u32[]{:S(2)}) async-start(bf16[8,10,32,512]{3,2,1,0:T(8,128)(2,1)} %shard_map.173.refs_3_), calls=%async_computation | async-start | bytes 5242880 | tf_op jit(solution)/shard_map/all_to_all | solution.py:681
  32.8 12.2 %shard_map.174 = (bf16[3,3696,128]{2,1,0:T(8,128)(2,1)}, bf16[3,3696,128]{2,1,0:T(8,128)(2,1)}, bf16[3,1856,128]{2,1,0:T(8,128)(2,1)}, bf16[3,1856,128]{2,1,0:T(8,128)(2,1)}) custom-call(s32[26]{0:T(128)} %concatenate.3.refs_1_.refs_0_, bf16[32,256,128]{2,1,0:T(8,128)(2,1)} %constant.59.clone.refs_1_, bf16[10,32,224,128]{3,2,1,0:T(8,128)(2,1)} %bitcast.27, ...), custom_call_target="tpu_custom_call" | custom-call | flops 1000 | bytes 1000 | tf_op jit(solution)/shard_map/pallas_call | solution.py:504
  46.2 1.8 collective-permute-start.8
  48.0 1.8 collective-permute-start.9
  49.8 9.2 %shard_map.175 = (bf16[2,3696,128]{2,1,0:T(8,128)(2,1)}, bf16[2,3696,128]{2,1,0:T(8,128)(2,1)}, bf16[2,1856,128]{2,1,0:T(8,128)(2,1)}, bf16[2,1856,128]{2,1,0:T(8,128)(2,1)}) custom-call(s32[26]{0:T(128)} %concatenate.3.refs_1_.refs_0_, bf16[32,256,128]{2,1,0:T(8,128)(2,1)} %constant.59.clone.refs_1_, bf16[10,32,224,128]{3,2,1,0:T(8,128)(2,1)} %bitcast.28, ...), custom_call_target="tpu_custom_call" | custom-call | flops 1000 | bytes 1000 | tf_op jit(solution)/shard_map/pallas_call | solution.py:504
  59.0 30.1 %all-to-all-done.refs_2_ = bf16[8,10,32,512]{3,2,1,0:T(8,128)(2,1)} async-done(((bf16[8,10,32,512]{3,2,1,0:T(8,128)(2,1)}), bf16[8,10,32,512]{3,2,1,0:T(8,128)(2,1)}, u32[]{:S(2)}, u32[]{:S(2)}) %all-to-all-start) | async-done | bytes 2621472 | tf_op jit(solution)/shard_map/all_to_all | solution.py:681
  89.1 10.2 %shard_map.176 = bf16[20,64,512]{2,1,0:T(8,128)(2,1)} custom-call(bf16[64,256]{1,0:T(8,128)(2,1)} %constant.60.clone.refs_0_, bf16[10,20,64,512]{3,2,1,0:T(8,128)(2,1)} %bitcast.30, bf16[8,10,32,512]{3,2,1,0:T(8,128)(2,1)} %all-to-all-done.refs_2_, bf16[2,3696,128]{2,1,0:T(8,128)(2,1)} %get-tuple-element.14.refs_3_.refs_1_), custom_call_target="tpu_custom_call" | custom-call | flops 1000 | bytes 1000 | tf_op jit(solution)/shard_map/pallas_call | solution.py:504
  99.2 2.2 dynamic-slice_bitcast_fusion
  101.5 8.4 %collective-permute-done.4.refs_2_.refs_7_ = bf16[3,3696,128]{2,1,0:T(8,128)(2,1)S(1)} collective-permute-done((bf16[3,3696,128]{2,1,0:T(8,128)(2,1)}, bf16[3,3696,128]{2,1,0:T(8,128)(2,1)S(1)}, u32[]{:S(2)}, u32[]{:S(2)}) %collective-permute-start.4) | collective-permute-done | bytes 2838560 | tf_op jit(solution)/shard_map/ppermute | solution.py:687
  109.9 1.6 copy-done.1
  111.6 2.3 shard_map.177.refs_1_
  115.0 1.6 collective-permute-start.11
  116.6 7.2 %shard_map.178.refs_5_.refs_1_ = bf16[8,10,32,512]{3,2,1,0:T(8,128)(2,1)} custom-call(bf16[256,64]{1,0:T(8,128)(2,1)} %constant.61.clone.refs_0_, bf16[10,64,512]{2,1,0:T(8,128)(2,1)} %shard_map.177.refs_1_), custom_call_target="tpu_custom_call" | custom-call | flops 1000 | bytes 1000 | tf_op jit(solution)/shard_map/pallas_call | solution.py:504
  125.9 6.0 %all-to-all-start.1 = ((bf16[8,10,32,512]{3,2,1,0:T(8,128)(2,1)}), bf16[8,10,32,512]{3,2,1,0:T(8,128)(2,1)S(1)}, u32[]{:S(2)}, u32[]{:S(2)}) async-start(bf16[8,10,32,512]{3,2,1,0:T(8,128)(2,1)} %shard_map.178.refs_5_.refs_1_), calls=%async_computation.1 | async-start | bytes 5242880 | tf_op jit(solution)/shard_map/all_to_all | solution.py:701
  133.1 2.3 reshape.22
  136.5 1.6 collective-permute-start.6
  138.1 1.7 collective-permute-start.7
  140.7 22.7 %shard_map.179.refs_4_.refs_6_ = bf16[10,32,224,128]{3,2,1,0:T(8,128)(2,1)} custom-call(bf16[160,160]{1,0:T(8,128)(2,1)} %get-tuple-element.26.refs_0_, bf16[160,160]{1,0:T(8,128)(2,1)} %get-tuple-element.25.refs_1_, f32[160,256]{1,0:T(8,128)} %broadcast_in_dim.21.refs_2_, bf16[10,32,224,128]{3,2,1,0:T(8,128)(2,1)} %bitcast.29, ...), custom_call_target="tpu_custom_call" | custom-call | flops 1000 | bytes 1000 | tf_op jit(solution)/shard_map/pallas_call | solution.py:504
  163.4 9.8 %collective-permute-done.5.refs_5_.refs_7_ = bf16[2,3696,128]{2,1,0:T(8,128)(2,1)} collective-permute-done((bf16[2,3696,128]{2,1,0:T(8,128)(2,1)}, bf16[2,3696,128]{2,1,0:T(8,128)(2,1)}, u32[]{:S(2)}, u32[]{:S(2)}) %collective-permute-start.5) | collective-permute-done | bytes 1892384 | tf_op jit(solution)/shard_map/ppermute | solution.py:687
  173.2 6.7 %shard_map.180.refs_4_ = bf16[3,3696,128]{2,1,0:T(8,128)(2,1)} custom-call(s32[26]{0:T(128)} %concatenate.3.refs_1_.refs_0_, bf16[3,3696,128]{2,1,0:T(8,128)(2,1)} %get-tuple-element.13.refs_3_.refs_1_, bf16[3,1856,128]{2,1,0:T(8,128)(2,1)} %collective-permute-done.8.refs_2_, bf16[3,1856,128]{2,1,0:T(8,128)(2,1)} %collective-permute-done.9.refs_3_, ...), custom_call_target="tpu_custom_call" | custom-call | flops 1000 | bytes 1000 | tf_op jit(solution)/shard_map/pallas_call | solution.py:504
  181.2 44.4 %all-gather.3.cloned.1.call-done = bf16[48,64,512]{2,1,0:T(8,128)(2,1)} async-done(((bf16[6,64,512]{2,1,0:T(8,128)(2,1)}), bf16[48,64,512]{2,1,0:T(8,128)(2,1)}) %all-gather.3.cloned.1.call-update) | async-done | bytes 3145744 | tf_op jit(solution)/shard_map/all_gather | solution.py:711
  225.6 3.1 slice.14
  228.7 19.2 %collective-permute-start.12 = (bf16[8,4,64,512]{3,2,1,0:T(8,128)(2,1)}, bf16[8,4,64,512]{3,2,1,0:T(8,128)(2,1)}, u32[]{:S(2)}, u32[]{:S(2)}) collective-permute-start(bf16[8,4,64,512]{3,2,1,0:T(8,128)(2,1)} %slice.14), channel_id=1, source_target_pairs={{16,0},{17,1},{18,2},{19,3},{20,4},{21,5},{22,6},{23,7},{24,8},{25... | collective-permute-start | bytes 6291464 | tf_op jit(solution)/shard_map/ppermute | solution.py:716
  248.0 4.6 %shard_map.181 = bf16[2,3696,128]{2,1,0:T(8,128)(2,1)} custom-call(s32[26]{0:T(128)} %concatenate.3.refs_1_.refs_0_, bf16[2,3696,128]{2,1,0:T(8,128)(2,1)} %get-tuple-element.14.refs_3_.refs_1_, bf16[2,1856,128]{2,1,0:T(8,128)(2,1)} %collective-permute-done.6.refs_2_, bf16[2,1856,128]{2,1,0:T(8,128)(2,1)} %collective-permute-done.7.refs_3_, ...), custom_call_target="tpu_custom_call" | custom-call | flops 1000 | bytes 1000 | tf_op jit(solution)/shard_map/pallas_call | solution.py:504
  253.9 1.4 constant_dynamic-slice_fusion.2
  255.2 1.5 copy-done
  256.8 34.7 %shard_map.183.refs_11_ = bf16[10,32,224,128]{3,2,1,0:T(8,128)(2,1)} custom-call(s32[26]{0:T(128)} %concatenate.3.refs_1_.refs_0_, bf16[128,256]{1,0:T(8,128)(2,1)} %constant.63.clone.refs_1_, bf16[128,256]{1,0:T(8,128)(2,1)} %constant.64.clone.refs_2_, bf16[96,64]{1,0:T(8,128)(2,1)} %bitcast.34, bf16[224,64]{1,0:T(8,128)(2,1)} %constant.65.clone.refs_4_, ...), custom_call_target="tpu_custom_call" | custom-call | flops 1000 | bytes 1000 | tf_op jit(solution)/shard_map/pallas_call | solution.py:504
  291.9 10.9 %collective-permute-done.10.refs_8_ = bf16[2,3696,128]{2,1,0:T(8,128)(2,1)} collective-permute-done((bf16[2,3696,128]{2,1,0:T(8,128)(2,1)}, bf16[2,3696,128]{2,1,0:T(8,128)(2,1)}, u32[]{:S(2)}, u32[]{:S(2)}) %collective-permute-start.10) | collective-permute-done | bytes 1892384 | tf_op jit(solution)/shard_map/ppermute | solution.py:715
  302.8 24.8 %shard_map.184 = bf16[10,32,224,128]{3,2,1,0:T(8,128)(2,1)} custom-call(s32[26]{0:T(128)} %concatenate.3.refs_1_.refs_0_, bf16[128,256]{1,0:T(8,128)(2,1)} %constant.63.clone.refs_1_, bf16[128,256]{1,0:T(8,128)(2,1)} %constant.64.clone.refs_2_, bf16[96,64]{1,0:T(8,128)(2,1)} %bitcast.35, ...), custom_call_target="tpu_custom_call", output_to_operand_aliasing={{}: (11, {})} | custom-call | flops 1000 | bytes 1000 | tf_op jit(solution)/shard_map/pallas_call | solution.py:504
  (48 shorter events, 11.5 us)
Async XLA Ops:
  6.5 133.4 %collective-permute-start.2 = (bf16[10,32,224,128]{3,2,1,0:T(8,128)(2,1)}, bf16[10,32,224,128]{3,2,1,0:T(8,128)(2,1)}, u32[]{:S(2)}, u32[]{:S(2)}) collective-permute-start(bf16[10,32,224,128]{3,2,1,0:T(8,128)(2,1)} %bitcast.25), channel_id=1, source_target_pairs={{0,1},{1,0},{2,3},{3,2},{4,5},{5,4},{6,7},{7,6},{8,9},{9,8},{10,11... | collective-permute-start | bytes 55050248 | tf_op jit(solution)/shard_map/ppermute | solution.py:31
  6.5 19.6 %copy-start.5 = (s32[1,8]{1,0:T(1,128)S(1)}, s32[1,8]{1,0:T(1,128)}, u32[]{:S(2)}) copy-start(s32[1,8]{1,0:T(1,128)} %param.22) | copy-start | bytes 100
  6.5 19.5 %collective-permute-start.1 = (s32[8]{0:T(128)}, s32[8]{0:T(128)S(1)}, u32[]{:S(2)}, u32[]{:S(2)}) collective-permute-start(s32[8]{0:T(128)} %bitcast.36), channel_id=1, source_target_pairs={{2,0},{4,2},{6,4},{8,6},{10,8},{12,10},{14,12},{3,1},{5,3},{7,5},{... | collective-permute-start | bytes 104 | tf_op jit(solution)/shard_map/ppermute | solution.py:25
  10.0 16.1 %collective-permute-start = (s32[8]{0:T(128)}, s32[8]{0:T(128)S(1)}, u32[]{:S(2)}, u32[]{:S(2)}) collective-permute-start(s32[8]{0:T(128)} %bitcast.37), channel_id=1, source_target_pairs={{0,2},{2,4},{4,6},{6,8},{8,10},{10,12},{12,14},{1,3},{3,5},{5,7},{... | collective-permute-start | bytes 104 | tf_op jit(solution)/shard_map/ppermute | solution.py:25
  26.7 62.4 %all-to-all-start = ((bf16[8,10,32,512]{3,2,1,0:T(8,128)(2,1)}), bf16[8,10,32,512]{3,2,1,0:T(8,128)(2,1)}, u32[]{:S(2)}, u32[]{:S(2)}) async-start(bf16[8,10,32,512]{3,2,1,0:T(8,128)(2,1)} %shard_map.173.refs_3_), calls=%async_computation | async-start | bytes 5242880 | tf_op jit(solution)/shard_map/all_to_all | solution.py:681
  32.8 192.8 %all-gather.3.cloned.1.call-start = ((), (), s32[]{:S(2)}) async-start(), calls=%async_computation.2 | async-start | bytes 3538944 | tf_op jit(solution)/shard_map/all_gather | solution.py:711
  45.0 64.9 %collective-permute-start.4 = (bf16[3,3696,128]{2,1,0:T(8,128)(2,1)}, bf16[3,3696,128]{2,1,0:T(8,128)(2,1)S(1)}, u32[]{:S(2)}, u32[]{:S(2)}) collective-permute-start(bf16[3,3696,128]{2,1,0:T(8,128)(2,1)} %get-tuple-element.15), channel_id=1, source_target_pairs={{0,16},{1,17},{2,18},{3,19},{4,20},{5,21},{6,22},{7,23},{8,24},{9,... | collective-permute-start | bytes 8515592 | tf_op jit(solution)/shard_map/ppermute | solution.py:687
  46.2 78.4 %collective-permute-start.8 = (bf16[3,1856,128]{2,1,0:T(8,128)(2,1)}, bf16[3,1856,128]{2,1,0:T(8,128)(2,1)}, u32[]{:S(2)}, u32[]{:S(2)}) collective-permute-start(bf16[3,1856,128]{2,1,0:T(8,128)(2,1)} %get-tuple-element.19), channel_id=1, source_target_pairs={{0,2},{2,4},{4,6},{6,8},{8,10},{10,12},{12,14},{1,3},{3,5},{5,7},{... | collective-permute-start | bytes 4276232 | tf_op jit(solution)/shard_map/ppermute | solution.py:690
  48.0 76.6 %collective-permute-start.9 = (bf16[3,1856,128]{2,1,0:T(8,128)(2,1)}, bf16[3,1856,128]{2,1,0:T(8,128)(2,1)}, u32[]{:S(2)}, u32[]{:S(2)}) collective-permute-start(bf16[3,1856,128]{2,1,0:T(8,128)(2,1)} %get-tuple-element.20), channel_id=1, source_target_pairs={{2,0},{4,2},{6,4},{8,6},{10,8},{12,10},{14,12},{3,1},{5,3},{7,5},{... | collective-permute-start | bytes 4276232 | tf_op jit(solution)/shard_map/ppermute | solution.py:691
  101.5 8.4 %collective-permute-start.3 = (bf16[10,64,512]{2,1,0:T(8,128)(2,1)S(1)}, bf16[10,64,512]{2,1,0:T(8,128)(2,1)S(1)}, u32[]{:S(2)}, u32[]{:S(2)}) collective-permute-start(bf16[10,64,512]{2,1,0:T(8,128)(2,1)S(1)} %get-tuple-element.21), channel_id=1, source_target_pairs={{0,1},{1,0},{2,3},{3,2},{4,5},{5,4},{6,7},{7,6},{8,9},{9,8},{10,11... | collective-permute-start | bytes 1966088 | tf_op jit(solution)/shard_map/ppermute | solution.py:31
  109.9 1.6 copy-start.1
  109.9 1.8 copy-start.3
  113.9 9.9 %copy-start.2 = (bf16[10,64,512]{2,1,0:T(8,128)(2,1)S(1)}, bf16[10,64,512]{2,1,0:T(8,128)(2,1)}, u32[]{:S(2)}) copy-start(bf16[10,64,512]{2,1,0:T(8,128)(2,1)} %shard_map.177.refs_1_) | copy-start | bytes 1966084
  115.0 8.8 %collective-permute-start.11 = (bf16[6,64,512]{2,1,0:T(8,128)(2,1)S(1)}, bf16[6,64,512]{2,1,0:T(8,128)(2,1)S(1)}, u32[]{:S(2)}, u32[]{:S(2)}) collective-permute-start(bf16[6,64,512]{2,1,0:T(8,128)(2,1)S(1)} %slice.12), channel_id=1, source_target_pairs={{16,0},{17,1},{18,2},{19,3},{20,4},{21,5},{22,6},{23,7},{24,8},{25... | collective-permute-start | bytes 1179656 | tf_op jit(solution)/shard_map/ppermute | solution.py:708
  124.6 7.3 %copy-start.4 = (bf16[1,20,10]{1,2,0:T(8,128)(2,1)S(1)}, bf16[1,20,10]{1,2,0:T(8,128)(2,1)}, u32[]{:S(2)}) copy-start(bf16[1,20,10]{1,2,0:T(8,128)(2,1)} %param.20) | copy-start | bytes 1204
  124.6 48.6 %collective-permute-start.5 = (bf16[2,3696,128]{2,1,0:T(8,128)(2,1)}, bf16[2,3696,128]{2,1,0:T(8,128)(2,1)}, u32[]{:S(2)}, u32[]{:S(2)}) collective-permute-start(bf16[2,3696,128]{2,1,0:T(8,128)(2,1)} %get-tuple-element.16), channel_id=1, source_target_pairs={{0,16},{1,17},{2,18},{3,19},{4,20},{5,21},{6,22},{7,23},{8,24},{9,... | collective-permute-start | bytes 5677064 | tf_op jit(solution)/shard_map/ppermute | solution.py:687
  125.9 129.3 %all-to-all-start.1 = ((bf16[8,10,32,512]{3,2,1,0:T(8,128)(2,1)}), bf16[8,10,32,512]{3,2,1,0:T(8,128)(2,1)S(1)}, u32[]{:S(2)}, u32[]{:S(2)}) async-start(bf16[8,10,32,512]{3,2,1,0:T(8,128)(2,1)} %shard_map.178.refs_5_.refs_1_), calls=%async_computation.1 | async-start | bytes 5242880 | tf_op jit(solution)/shard_map/all_to_all | solution.py:701
  131.9 7.9 %copy-start.6 = (bf16[1,10]{1,0:T(2,128)(2,1)S(1)}, bf16[1,10]{1,0:T(2,128)(2,1)}, u32[]{:S(2)}) copy-start(bf16[1,10]{1,0:T(2,128)(2,1)} %param.21) | copy-start | bytes 64
  136.5 111.4 %collective-permute-start.6 = (bf16[2,1856,128]{2,1,0:T(8,128)(2,1)}, bf16[2,1856,128]{2,1,0:T(8,128)(2,1)}, u32[]{:S(2)}, u32[]{:S(2)}) collective-permute-start(bf16[2,1856,128]{2,1,0:T(8,128)(2,1)} %get-tuple-element.17), channel_id=1, source_target_pairs={{0,2},{2,4},{4,6},{6,8},{8,10},{10,12},{12,14},{1,3},{3,5},{5,7},{... | collective-permute-start | bytes 2850824 | tf_op jit(solution)/shard_map/ppermute | solution.py:690
  138.1 109.8 %collective-permute-start.7 = (bf16[2,1856,128]{2,1,0:T(8,128)(2,1)}, bf16[2,1856,128]{2,1,0:T(8,128)(2,1)}, u32[]{:S(2)}, u32[]{:S(2)}) collective-permute-start(bf16[2,1856,128]{2,1,0:T(8,128)(2,1)} %get-tuple-element.18), channel_id=1, source_target_pairs={{2,0},{4,2},{6,4},{8,6},{10,8},{12,10},{14,12},{3,1},{5,3},{7,5},{... | collective-permute-start | bytes 2850824 | tf_op jit(solution)/shard_map/ppermute | solution.py:691
  179.9 75.4 %collective-permute-start.13 = (bf16[3,3696,128]{2,1,0:T(8,128)(2,1)}, bf16[3,3696,128]{2,1,0:T(8,128)(2,1)}, u32[]{:S(2)}, u32[]{:S(2)}) collective-permute-start(bf16[3,3696,128]{2,1,0:T(8,128)(2,1)} %shard_map.180.refs_4_), channel_id=1, source_target_pairs={{0,16},{1,17},{2,18},{3,19},{4,20},{5,21},{6,22},{7,23},{8,24},{9,... | collective-permute-start | bytes 8515592 | tf_op jit(solution)/shard_map/ppermute | solution.py:715
  228.7 63.2 %collective-permute-start.12 = (bf16[8,4,64,512]{3,2,1,0:T(8,128)(2,1)}, bf16[8,4,64,512]{3,2,1,0:T(8,128)(2,1)}, u32[]{:S(2)}, u32[]{:S(2)}) collective-permute-start(bf16[8,4,64,512]{3,2,1,0:T(8,128)(2,1)} %slice.14), channel_id=1, source_target_pairs={{16,0},{17,1},{18,2},{19,3},{20,4},{21,5},{22,6},{23,7},{24,8},{25... | collective-permute-start | bytes 6291464 | tf_op jit(solution)/shard_map/ppermute | solution.py:716
  252.6 50.2 %collective-permute-start.10 = (bf16[2,3696,128]{2,1,0:T(8,128)(2,1)}, bf16[2,3696,128]{2,1,0:T(8,128)(2,1)}, u32[]{:S(2)}, u32[]{:S(2)}) collective-permute-start(bf16[2,3696,128]{2,1,0:T(8,128)(2,1)} %shard_map.181), channel_id=1, source_target_pairs={{0,16},{1,17},{2,18},{3,19},{4,20},{5,21},{6,22},{7,23},{8,24},{9,... | collective-permute-start | bytes 5677064 | tf_op jit(solution)/shard_map/ppermute | solution.py:715
  255.2 1.5 copy-start
Sparse Core Ops, SparseCore 0:
  124.7 100.7 all-gather.2

commit v4 on v3

--- a/solution.py
+++ b/solution.py
@@ -360,7 +360,7 @@
 
     start = pl.multiple_of(step * rows, rows)
 
-    @pl.loop(0, plan.outs)
+    @pl.loop(0, plan.outs, unroll=4)
     def _(o):
         total = weights[0, o].astype(F32) * coeffs[0, pl.ds(start, rows), :]
         for c in range(1, ch):

time: 336 us -> 336 us (level)
  no operation moved by 1% of the time
where the time goes in v4:
time: 336 us; the launch traced here: 334 us
  Pallas kernels  148 us (44%)
  waiting for transfers between devices  104 us (31%)
  starting transfers between devices  51.3 us (15%)
  local copies, waits for them, and re-layouts  16 us (5%)
  between operations  13.6 us (4%)
    pallas_call x11, Pallas kernels, call(): pl.pallas_call(run, grid=grid, in_specs=in_specs + [pl.BlockSpec(memory_s...  148 us
    all_gather x1, waiting for transfers between devices, fast_body(): here = lax.all_gather(here, 'slab', axis=0, tiled=False)  43.9 us
    all_to_all x1, waiting for transfers between devices, fast_body(): lax.all_to_all(sent, 'slab', split_axis=0, concat_axis=0, tiled=True)  30.1 us
    ppermute x1, starting transfers between devices, fast_body(): gathered = [here, lax.ppermute(here[:, lead - rest:], 'pool', [(1, 0)])]  19.8 us
    ppermute x2, waiting for transfers between devices, fast_body(): firsts.append(lax.ppermute(lead, 'pool', [(0, 1)]))  18.6 us
    ppermute x2, waiting for transfers between devices, fast_body(): seconds.append(lax.ppermute(last, 'pool', [(0, 1)]))  10.9 us
  transfers between devices with their start and end apart: 17, of which 6 were waited for; matrix products, arithmetic and copies ran while one was open for 4% of the time, Pallas kernels for 37%

profile of v4, /device:TPU:18, one launch (start us, length us, event | category | flops | bytes accessed | tf_op | source)
XLA Modules:
  0.0 334.4 jit_solution(1221677077884498868)
XLA Ops:
  6.5 3.4 %collective-permute-start.1 = (s32[8]{0:T(128)}, s32[8]{0:T(128)S(1)}, u32[]{:S(2)}, u32[]{:S(2)}) collective-permute-start(s32[8]{0:T(128)} %bitcast.36), channel_id=1, source_target_pairs={{2,0},{4,2},{6,4},{8,6},{10,8},{12,10},{14,12},{3,1},{5,3},{7,5},{... | collective-permute-start | bytes 104 | tf_op jit(solution)/shard_map/ppermute | solution.py:25
  10.0 2.5 collective-permute-start
  12.5 13.6 %shard_map.172.refs_0_ = bf16[8,10,32,512]{3,2,1,0:T(8,128)(2,1)} custom-call(bf16[64,224]{1,0:T(8,128)(2,1)} %constant.57.clone.refs_0_, bf16[256,128]{1,0:T(8,128)(2,1)} %constant.58.clone.refs_1_, bf16[10,32,224,128]{3,2,1,0:T(8,128)(2,1)} %bitcast.26), custom_call_target="tpu_custom_call" | custom-call | flops 1000 | bytes 1000 | tf_op jit(solution)/shard_map/pallas_call | solution.py:504
  26.7 6.0 %all-to-all-start = ((bf16[8,10,32,512]{3,2,1,0:T(8,128)(2,1)}), bf16[8,10,32,512]{3,2,1,0:T(8,128)(2,1)}, u32[]{:S(2)}, u32[]{:S(2)}) async-start(bf16[8,10,32,512]{3,2,1,0:T(8,128)(2,1)} %shard_map.173.refs_3_), calls=%async_computation | async-start | bytes 5242880 | tf_op jit(solution)/shard_map/all_to_all | solution.py:681
  32.8 12.2 %shard_map.174 = (bf16[3,3696,128]{2,1,0:T(8,128)(2,1)}, bf16[3,3696,128]{2,1,0:T(8,128)(2,1)}, bf16[3,1856,128]{2,1,0:T(8,128)(2,1)}, bf16[3,1856,128]{2,1,0:T(8,128)(2,1)}) custom-call(s32[26]{0:T(128)} %concatenate.3.refs_1_.refs_0_, bf16[32,256,128]{2,1,0:T(8,128)(2,1)} %constant.59.clone.refs_1_, bf16[10,32,224,128]{3,2,1,0:T(8,128)(2,1)} %bitcast.27, ...), custom_call_target="tpu_custom_call" | custom-call | flops 1000 | bytes 1000 | tf_op jit(solution)/shard_map/pallas_call | solution.py:504
  46.2 1.8 collective-permute-start.8
  48.0 1.8 collective-permute-start.9
  49.8 9.2 %shard_map.175 = (bf16[2,3696,128]{2,1,0:T(8,128)(2,1)}, bf16[2,3696,128]{2,1,0:T(8,128)(2,1)}, bf16[2,1856,128]{2,1,0:T(8,128)(2,1)}, bf16[2,1856,128]{2,1,0:T(8,128)(2,1)}) custom-call(s32[26]{0:T(128)} %concatenate.3.refs_1_.refs_0_, bf16[32,256,128]{2,1,0:T(8,128)(2,1)} %constant.59.clone.refs_1_, bf16[10,32,224,128]{3,2,1,0:T(8,128)(2,1)} %bitcast.28, ...), custom_call_target="tpu_custom_call" | custom-call | flops 1000 | bytes 1000 | tf_op jit(solution)/shard_map/pallas_call | solution.py:504
  59.0 30.1 %all-to-all-done.refs_2_ = bf16[8,10,32,512]{3,2,1,0:T(8,128)(2,1)} async-done(((bf16[8,10,32,512]{3,2,1,0:T(8,128)(2,1)}), bf16[8,10,32,512]{3,2,1,0:T(8,128)(2,1)}, u32[]{:S(2)}, u32[]{:S(2)}) %all-to-all-start) | async-done | bytes 2621472 | tf_op jit(solution)/shard_map/all_to_all | solution.py:681
  89.1 9.8 %shard_map.176 = bf16[20,64,512]{2,1,0:T(8,128)(2,1)} custom-call(bf16[64,256]{1,0:T(8,128)(2,1)} %constant.60.clone.refs_0_, bf16[10,20,64,512]{3,2,1,0:T(8,128)(2,1)} %bitcast.30, bf16[8,10,32,512]{3,2,1,0:T(8,128)(2,1)} %all-to-all-done.refs_2_, bf16[2,3696,128]{2,1,0:T(8,128)(2,1)} %get-tuple-element.14.refs_3_.refs_1_), custom_call_target="tpu_custom_call" | custom-call | flops 1000 | bytes 1000 | tf_op jit(solution)/shard_map/pallas_call | solution.py:504
  98.9 2.2 dynamic-slice_bitcast_fusion
  101.1 8.7 %collective-permute-done.4.refs_2_.refs_7_ = bf16[3,3696,128]{2,1,0:T(8,128)(2,1)S(1)} collective-permute-done((bf16[3,3696,128]{2,1,0:T(8,128)(2,1)}, bf16[3,3696,128]{2,1,0:T(8,128)(2,1)S(1)}, u32[]{:S(2)}, u32[]{:S(2)}) %collective-permute-start.4) | collective-permute-done | bytes 2838560 | tf_op jit(solution)/shard_map/ppermute | solution.py:687
  109.9 1.6 copy-done.1
  111.6 2.3 shard_map.177.refs_1_
  115.0 1.6 collective-permute-start.11
  116.6 7.2 %shard_map.178.refs_5_.refs_1_ = bf16[8,10,32,512]{3,2,1,0:T(8,128)(2,1)} custom-call(bf16[256,64]{1,0:T(8,128)(2,1)} %constant.61.clone.refs_0_, bf16[10,64,512]{2,1,0:T(8,128)(2,1)} %shard_map.177.refs_1_), custom_call_target="tpu_custom_call" | custom-call | flops 1000 | bytes 1000 | tf_op jit(solution)/shard_map/pallas_call | solution.py:504
  125.9 6.0 %all-to-all-start.1 = ((bf16[8,10,32,512]{3,2,1,0:T(8,128)(2,1)}), bf16[8,10,32,512]{3,2,1,0:T(8,128)(2,1)S(1)}, u32[]{:S(2)}, u32[]{:S(2)}) async-start(bf16[8,10,32,512]{3,2,1,0:T(8,128)(2,1)} %shard_map.178.refs_5_.refs_1_), calls=%async_computation.1 | async-start | bytes 5242880 | tf_op jit(solution)/shard_map/all_to_all | solution.py:701
  133.1 2.3 reshape.22
  136.5 1.6 collective-permute-start.6
  138.1 1.7 collective-permute-start.7
  140.7 22.7 %shard_map.179.refs_4_.refs_6_ = bf16[10,32,224,128]{3,2,1,0:T(8,128)(2,1)} custom-call(bf16[160,160]{1,0:T(8,128)(2,1)} %get-tuple-element.26.refs_0_, bf16[160,160]{1,0:T(8,128)(2,1)} %get-tuple-element.25.refs_1_, f32[160,256]{1,0:T(8,128)} %broadcast_in_dim.21.refs_2_, bf16[10,32,224,128]{3,2,1,0:T(8,128)(2,1)} %bitcast.29, ...), custom_call_target="tpu_custom_call" | custom-call | flops 1000 | bytes 1000 | tf_op jit(solution)/shard_map/pallas_call | solution.py:504
  163.4 9.8 %collective-permute-done.5.refs_5_.refs_7_ = bf16[2,3696,128]{2,1,0:T(8,128)(2,1)} collective-permute-done((bf16[2,3696,128]{2,1,0:T(8,128)(2,1)}, bf16[2,3696,128]{2,1,0:T(8,128)(2,1)}, u32[]{:S(2)}, u32[]{:S(2)}) %collective-permute-start.5) | collective-permute-done | bytes 1892384 | tf_op jit(solution)/shard_map/ppermute | solution.py:687
  173.2 6.7 %shard_map.180.refs_4_ = bf16[3,3696,128]{2,1,0:T(8,128)(2,1)} custom-call(s32[26]{0:T(128)} %concatenate.3.refs_1_.refs_0_, bf16[3,3696,128]{2,1,0:T(8,128)(2,1)} %get-tuple-element.13.refs_3_.refs_1_, bf16[3,1856,128]{2,1,0:T(8,128)(2,1)} %collective-permute-done.8.refs_2_, bf16[3,1856,128]{2,1,0:T(8,128)(2,1)} %collective-permute-done.9.refs_3_, ...), custom_call_target="tpu_custom_call" | custom-call | flops 1000 | bytes 1000 | tf_op jit(solution)/shard_map/pallas_call | solution.py:504
  181.2 43.9 %all-gather.3.cloned.1.call-done = bf16[48,64,512]{2,1,0:T(8,128)(2,1)} async-done(((bf16[6,64,512]{2,1,0:T(8,128)(2,1)}), bf16[48,64,512]{2,1,0:T(8,128)(2,1)}) %all-gather.3.cloned.1.call-update) | async-done | bytes 3145744 | tf_op jit(solution)/shard_map/all_gather | solution.py:711
  225.1 3.1 slice.14
  228.2 19.8 %collective-permute-start.12 = (bf16[8,4,64,512]{3,2,1,0:T(8,128)(2,1)}, bf16[8,4,64,512]{3,2,1,0:T(8,128)(2,1)}, u32[]{:S(2)}, u32[]{:S(2)}) collective-permute-start(bf16[8,4,64,512]{3,2,1,0:T(8,128)(2,1)} %slice.14), channel_id=1, source_target_pairs={{16,0},{17,1},{18,2},{19,3},{20,4},{21,5},{22,6},{23,7},{24,8},{25... | collective-permute-start | bytes 6291464 | tf_op jit(solution)/shard_map/ppermute | solution.py:716
  248.0 4.6 %shard_map.181 = bf16[2,3696,128]{2,1,0:T(8,128)(2,1)} custom-call(s32[26]{0:T(128)} %concatenate.3.refs_1_.refs_0_, bf16[2,3696,128]{2,1,0:T(8,128)(2,1)} %get-tuple-element.14.refs_3_.refs_1_, bf16[2,1856,128]{2,1,0:T(8,128)(2,1)} %collective-permute-done.6.refs_2_, bf16[2,1856,128]{2,1,0:T(8,128)(2,1)} %collective-permute-done.7.refs_3_, ...), custom_call_target="tpu_custom_call" | custom-call | flops 1000 | bytes 1000 | tf_op jit(solution)/shard_map/pallas_call | solution.py:504
  253.9 1.4 constant_dynamic-slice_fusion.2
  255.2 1.5 copy-done
  256.8 34.7 %shard_map.183.refs_11_ = bf16[10,32,224,128]{3,2,1,0:T(8,128)(2,1)} custom-call(s32[26]{0:T(128)} %concatenate.3.refs_1_.refs_0_, bf16[128,256]{1,0:T(8,128)(2,1)} %constant.63.clone.refs_1_, bf16[128,256]{1,0:T(8,128)(2,1)} %constant.64.clone.refs_2_, bf16[96,64]{1,0:T(8,128)(2,1)} %bitcast.34, bf16[224,64]{1,0:T(8,128)(2,1)} %constant.65.clone.refs_4_, ...), custom_call_target="tpu_custom_call" | custom-call | flops 1000 | bytes 1000 | tf_op jit(solution)/shard_map/pallas_call | solution.py:504
  291.9 10.9 %collective-permute-done.10.refs_8_ = bf16[2,3696,128]{2,1,0:T(8,128)(2,1)} collective-permute-done((bf16[2,3696,128]{2,1,0:T(8,128)(2,1)}, bf16[2,3696,128]{2,1,0:T(8,128)(2,1)}, u32[]{:S(2)}, u32[]{:S(2)}) %collective-permute-start.10) | collective-permute-done | bytes 1892384 | tf_op jit(solution)/shard_map/ppermute | solution.py:715
  302.8 24.8 %shard_map.184 = bf16[10,32,224,128]{3,2,1,0:T(8,128)(2,1)} custom-call(s32[26]{0:T(128)} %concatenate.3.refs_1_.refs_0_, bf16[128,256]{1,0:T(8,128)(2,1)} %constant.63.clone.refs_1_, bf16[128,256]{1,0:T(8,128)(2,1)} %constant.64.clone.refs_2_, bf16[96,64]{1,0:T(8,128)(2,1)} %bitcast.35, ...), custom_call_target="tpu_custom_call", output_to_operand_aliasing={{}: (11, {})} | custom-call | flops 1000 | bytes 1000 | tf_op jit(solution)/shard_map/pallas_call | solution.py:504
  (48 shorter events, 11.5 us)
Async XLA Ops:
  6.5 133.4 %collective-permute-start.2 = (bf16[10,32,224,128]{3,2,1,0:T(8,128)(2,1)}, bf16[10,32,224,128]{3,2,1,0:T(8,128)(2,1)}, u32[]{:S(2)}, u32[]{:S(2)}) collective-permute-start(bf16[10,32,224,128]{3,2,1,0:T(8,128)(2,1)} %bitcast.25), channel_id=1, source_target_pairs={{0,1},{1,0},{2,3},{3,2},{4,5},{5,4},{6,7},{7,6},{8,9},{9,8},{10,11... | collective-permute-start | bytes 55050248 | tf_op jit(solution)/shard_map/ppermute | solution.py:31
  6.5 19.6 %copy-start.5 = (s32[1,8]{1,0:T(1,128)S(1)}, s32[1,8]{1,0:T(1,128)}, u32[]{:S(2)}) copy-start(s32[1,8]{1,0:T(1,128)} %param.22) | copy-start | bytes 100
  6.5 19.5 %collective-permute-start.1 = (s32[8]{0:T(128)}, s32[8]{0:T(128)S(1)}, u32[]{:S(2)}, u32[]{:S(2)}) collective-permute-start(s32[8]{0:T(128)} %bitcast.36), channel_id=1, source_target_pairs={{2,0},{4,2},{6,4},{8,6},{10,8},{12,10},{14,12},{3,1},{5,3},{7,5},{... | collective-permute-start | bytes 104 | tf_op jit(solution)/shard_map/ppermute | solution.py:25
  10.0 16.1 %collective-permute-start = (s32[8]{0:T(128)}, s32[8]{0:T(128)S(1)}, u32[]{:S(2)}, u32[]{:S(2)}) collective-permute-start(s32[8]{0:T(128)} %bitcast.37), channel_id=1, source_target_pairs={{0,2},{2,4},{4,6},{6,8},{8,10},{10,12},{12,14},{1,3},{3,5},{5,7},{... | collective-permute-start | bytes 104 | tf_op jit(solution)/shard_map/ppermute | solution.py:25
  26.7 62.4 %all-to-all-start = ((bf16[8,10,32,512]{3,2,1,0:T(8,128)(2,1)}), bf16[8,10,32,512]{3,2,1,0:T(8,128)(2,1)}, u32[]{:S(2)}, u32[]{:S(2)}) async-start(bf16[8,10,32,512]{3,2,1,0:T(8,128)(2,1)} %shard_map.173.refs_3_), calls=%async_computation | async-start | bytes 5242880 | tf_op jit(solution)/shard_map/all_to_all | solution.py:681
  32.8 192.3 %all-gather.3.cloned.1.call-start = ((), (), s32[]{:S(2)}) async-start(), calls=%async_computation.2 | async-start | bytes 3538944 | tf_op jit(solution)/shard_map/all_gather | solution.py:711
  45.0 64.9 %collective-permute-start.4 = (bf16[3,3696,128]{2,1,0:T(8,128)(2,1)}, bf16[3,3696,128]{2,1,0:T(8,128)(2,1)S(1)}, u32[]{:S(2)}, u32[]{:S(2)}) collective-permute-start(bf16[3,3696,128]{2,1,0:T(8,128)(2,1)} %get-tuple-element.15), channel_id=1, source_target_pairs={{0,16},{1,17},{2,18},{3,19},{4,20},{5,21},{6,22},{7,23},{8,24},{9,... | collective-permute-start | bytes 8515592 | tf_op jit(solution)/shard_map/ppermute | solution.py:687
  46.2 78.4 %collective-permute-start.8 = (bf16[3,1856,128]{2,1,0:T(8,128)(2,1)}, bf16[3,1856,128]{2,1,0:T(8,128)(2,1)}, u32[]{:S(2)}, u32[]{:S(2)}) collective-permute-start(bf16[3,1856,128]{2,1,0:T(8,128)(2,1)} %get-tuple-element.19), channel_id=1, source_target_pairs={{0,2},{2,4},{4,6},{6,8},{8,10},{10,12},{12,14},{1,3},{3,5},{5,7},{... | collective-permute-start | bytes 4276232 | tf_op jit(solution)/shard_map/ppermute | solution.py:690
  48.0 76.6 %collective-permute-start.9 = (bf16[3,1856,128]{2,1,0:T(8,128)(2,1)}, bf16[3,1856,128]{2,1,0:T(8,128)(2,1)}, u32[]{:S(2)}, u32[]{:S(2)}) collective-permute-start(bf16[3,1856,128]{2,1,0:T(8,128)(2,1)} %get-tuple-element.20), channel_id=1, source_target_pairs={{2,0},{4,2},{6,4},{8,6},{10,8},{12,10},{14,12},{3,1},{5,3},{7,5},{... | collective-permute-start | bytes 4276232 | tf_op jit(solution)/shard_map/ppermute | solution.py:691
  101.1 8.7 %collective-permute-start.3 = (bf16[10,64,512]{2,1,0:T(8,128)(2,1)S(1)}, bf16[10,64,512]{2,1,0:T(8,128)(2,1)S(1)}, u32[]{:S(2)}, u32[]{:S(2)}) collective-permute-start(bf16[10,64,512]{2,1,0:T(8,128)(2,1)S(1)} %get-tuple-element.21), channel_id=1, source_target_pairs={{0,1},{1,0},{2,3},{3,2},{4,5},{5,4},{6,7},{7,6},{8,9},{9,8},{10,11... | collective-permute-start | bytes 1966088 | tf_op jit(solution)/shard_map/ppermute | solution.py:31
  109.9 1.6 copy-start.1
  109.9 1.8 copy-start.3
  113.9 9.9 %copy-start.2 = (bf16[10,64,512]{2,1,0:T(8,128)(2,1)S(1)}, bf16[10,64,512]{2,1,0:T(8,128)(2,1)}, u32[]{:S(2)}) copy-start(bf16[10,64,512]{2,1,0:T(8,128)(2,1)} %shard_map.177.refs_1_) | copy-start | bytes 1966084
  115.0 8.8 %collective-permute-start.11 = (bf16[6,64,512]{2,1,0:T(8,128)(2,1)S(1)}, bf16[6,64,512]{2,1,0:T(8,128)(2,1)S(1)}, u32[]{:S(2)}, u32[]{:S(2)}) collective-permute-start(bf16[6,64,512]{2,1,0:T(8,128)(2,1)S(1)} %slice.12), channel_id=1, source_target_pairs={{16,0},{17,1},{18,2},{19,3},{20,4},{21,5},{22,6},{23,7},{24,8},{25... | collective-permute-start | bytes 1179656 | tf_op jit(solution)/shard_map/ppermute | solution.py:708
  124.6 7.3 %copy-start.4 = (bf16[1,20,10]{1,2,0:T(8,128)(2,1)S(1)}, bf16[1,20,10]{1,2,0:T(8,128)(2,1)}, u32[]{:S(2)}) copy-start(bf16[1,20,10]{1,2,0:T(8,128)(2,1)} %param.20) | copy-start | bytes 1204
  124.6 48.6 %collective-permute-start.5 = (bf16[2,3696,128]{2,1,0:T(8,128)(2,1)}, bf16[2,3696,128]{2,1,0:T(8,128)(2,1)}, u32[]{:S(2)}, u32[]{:S(2)}) collective-permute-start(bf16[2,3696,128]{2,1,0:T(8,128)(2,1)} %get-tuple-element.16), channel_id=1, source_target_pairs={{0,16},{1,17},{2,18},{3,19},{4,20},{5,21},{6,22},{7,23},{8,24},{9,... | collective-permute-start | bytes 5677064 | tf_op jit(solution)/shard_map/ppermute | solution.py:687
  125.9 129.3 %all-to-all-start.1 = ((bf16[8,10,32,512]{3,2,1,0:T(8,128)(2,1)}), bf16[8,10,32,512]{3,2,1,0:T(8,128)(2,1)S(1)}, u32[]{:S(2)}, u32[]{:S(2)}) async-start(bf16[8,10,32,512]{3,2,1,0:T(8,128)(2,1)} %shard_map.178.refs_5_.refs_1_), calls=%async_computation.1 | async-start | bytes 5242880 | tf_op jit(solution)/shard_map/all_to_all | solution.py:701
  131.9 7.9 %copy-start.6 = (bf16[1,10]{1,0:T(2,128)(2,1)S(1)}, bf16[1,10]{1,0:T(2,128)(2,1)}, u32[]{:S(2)}) copy-start(bf16[1,10]{1,0:T(2,128)(2,1)} %param.21) | copy-start | bytes 64
  136.5 111.4 %collective-permute-start.6 = (bf16[2,1856,128]{2,1,0:T(8,128)(2,1)}, bf16[2,1856,128]{2,1,0:T(8,128)(2,1)}, u32[]{:S(2)}, u32[]{:S(2)}) collective-permute-start(bf16[2,1856,128]{2,1,0:T(8,128)(2,1)} %get-tuple-element.17), channel_id=1, source_target_pairs={{0,2},{2,4},{4,6},{6,8},{8,10},{10,12},{12,14},{1,3},{3,5},{5,7},{... | collective-permute-start | bytes 2850824 | tf_op jit(solution)/shard_map/ppermute | solution.py:690
  138.1 109.8 %collective-permute-start.7 = (bf16[2,1856,128]{2,1,0:T(8,128)(2,1)}, bf16[2,1856,128]{2,1,0:T(8,128)(2,1)}, u32[]{:S(2)}, u32[]{:S(2)}) collective-permute-start(bf16[2,1856,128]{2,1,0:T(8,128)(2,1)} %get-tuple-element.18), channel_id=1, source_target_pairs={{2,0},{4,2},{6,4},{8,6},{10,8},{12,10},{14,12},{3,1},{5,3},{7,5},{... | collective-permute-start | bytes 2850824 | tf_op jit(solution)/shard_map/ppermute | solution.py:691
  179.9 75.4 %collective-permute-start.13 = (bf16[3,3696,128]{2,1,0:T(8,128)(2,1)}, bf16[3,3696,128]{2,1,0:T(8,128)(2,1)}, u32[]{:S(2)}, u32[]{:S(2)}) collective-permute-start(bf16[3,3696,128]{2,1,0:T(8,128)(2,1)} %shard_map.180.refs_4_), channel_id=1, source_target_pairs={{0,16},{1,17},{2,18},{3,19},{4,20},{5,21},{6,22},{7,23},{8,24},{9,... | collective-permute-start | bytes 8515592 | tf_op jit(solution)/shard_map/ppermute | solution.py:715
  228.2 63.7 %collective-permute-start.12 = (bf16[8,4,64,512]{3,2,1,0:T(8,128)(2,1)}, bf16[8,4,64,512]{3,2,1,0:T(8,128)(2,1)}, u32[]{:S(2)}, u32[]{:S(2)}) collective-permute-start(bf16[8,4,64,512]{3,2,1,0:T(8,128)(2,1)} %slice.14), channel_id=1, source_target_pairs={{16,0},{17,1},{18,2},{19,3},{20,4},{21,5},{22,6},{23,7},{24,8},{25... | collective-permute-start | bytes 6291464 | tf_op jit(solution)/shard_map/ppermute | solution.py:716
  252.6 50.2 %collective-permute-start.10 = (bf16[2,3696,128]{2,1,0:T(8,128)(2,1)}, bf16[2,3696,128]{2,1,0:T(8,128)(2,1)}, u32[]{:S(2)}, u32[]{:S(2)}) collective-permute-start(bf16[2,3696,128]{2,1,0:T(8,128)(2,1)} %shard_map.181), channel_id=1, source_target_pairs={{0,16},{1,17},{2,18},{3,19},{4,20},{5,21},{6,22},{7,23},{8,24},{9,... | collective-permute-start | bytes 5677064 | tf_op jit(solution)/shard_map/ppermute | solution.py:715
  255.2 1.5 copy-start
Sparse Core Ops, SparseCore 0:
  124.7 100.2 all-gather.2
